TPU v7x, 32 devices: a whole 2x2x4 slice. The times are simulated.
32 devices in a mesh: gx: 4 (over y, core), gy: 2 (over x), gz: 4 (over z).
Axes of the slice: x: 2, y: 2, z: 4, core: 2. Of those that a mesh axis runs over, the one named last changes fastest.
Arguments:
- fields: float32 [6, 16, 64, 256], P(None, 'gz', 'gx', 'gy'), may hold values from -6 to 6
- material: int32 [16, 64, 256], P('gz', 'gx', 'gy'), may hold values from 0 to 15
- faces: int32 [3, 16, 64, 256], P(None, 'gz', 'gx', 'gy'), may hold values 0 or 1
- permittivity: float32 [16], replicated, may hold values from 1 to 8
- losses: float32 [16], replicated, may hold values from 0.02 to 1
- angles: float32 [2, 512], replicated, may hold values from -3.140625 to 3.140625
- wavenumbers: float32 [4], replicated, may hold values from 0.2 to 1.6
Outputs:
- fields_next: float32 [6, 16, 64, 256], P(None, 'gz', 'gx', 'gy')
- far_field: float32 [512, 96], P(('gx', 'gy', 'gz'))
Inputs may be any that keep to these rules, and one draw needn't show every extreme that they name: material indices into the tables. `faces`: 1 where a cell lies on the face of that normal, else 0.
All inputs are finite; a program needn't handle non-finite values. No bound on the sum of `faces` on one device may be relied on, other than what follows from the above.
Results may differ from a plain program's by a relative error of at most 0.0038.
Values may be sent and summed in bfloat16 or wider, within the bound.
A program may use at most 64 MiB of HBM per device.

v0:
```python
import math

import jax
import jax.numpy as jnp
from jax import lax
from jax.sharding import PartitionSpec as P

DIR_DEV = 16


COURANT = 0.5


def passed_along(shard, axis, by):
    devices = lax.axis_size(axis)
    pairs = [(i, i + by) for i in range(devices) if 0 <= i + by < devices]
    return lax.ppermute(shard, axis, pairs)


def ahead_with(field, axis, following):
    count = field.shape[axis]
    later = lax.slice_in_dim(field, 1, count, axis=axis)
    return jnp.concatenate([later, following], axis=axis) - field


def behind_with(field, axis, preceding):
    count = field.shape[axis]
    earlier = lax.slice_in_dim(field, 0, count - 1, axis=axis)
    return field - jnp.concatenate([preceding, earlier], axis=axis)


def curl_forward(electric):
    next_z = passed_along(electric[0:2, 0:1], "gz", -1)
    next_x = passed_along(electric[1:3, :, 0:1], "gx", -1)
    pair_y = jnp.stack([electric[0], electric[2]])
    next_y = passed_along(pair_y[:, :, :, 0:1], "gy", -1)
    return jnp.stack(
        [
            ahead_with(electric[2], 2, next_y[1]) - ahead_with(electric[1], 0, next_z[1]),
            ahead_with(electric[0], 0, next_z[0]) - ahead_with(electric[2], 1, next_x[1]),
            ahead_with(electric[1], 1, next_x[0]) - ahead_with(electric[0], 2, next_y[0]),
        ]
    )


def curl_backward(magnetic):
    prev_z = passed_along(magnetic[0:2, -1:], "gz", 1)
    prev_x = passed_along(magnetic[1:3, :, -1:], "gx", 1)
    pair_y = jnp.stack([magnetic[0], magnetic[2]])
    prev_y = passed_along(pair_y[:, :, :, -1:], "gy", 1)
    return jnp.stack(
        [
            behind_with(magnetic[2], 2, prev_y[1]) - behind_with(magnetic[1], 0, prev_z[1]),
            behind_with(magnetic[0], 0, prev_z[0]) - behind_with(magnetic[2], 1, prev_x[1]),
            behind_with(magnetic[1], 1, prev_x[0]) - behind_with(magnetic[0], 2, prev_y[0]),
        ]
    )


def surface_rows(state, faces):
    masks = faces.astype(jnp.float32)
    normal_x = masks[0]
    normal_y = masks[1]
    normal_z = masks[2]
    channels = jnp.stack(
        [
            -state[5] * normal_x,
            state[4] * normal_x,
            state[2] * normal_x,
            -state[1] * normal_x,
            state[5] * normal_y,
            -state[3] * normal_y,
            -state[2] * normal_y,
            state[0] * normal_y,
            -state[4] * normal_z,
            state[3] * normal_z,
            state[1] * normal_z,
            -state[0] * normal_z,
        ]
    )
    depth, width, height = (channels.shape[1], channels.shape[2], channels.shape[3])
    shaped = channels.reshape(12, depth // 4, 4, width // 4, 4, height // 4, 4)
    return jnp.mean(shaped, axis=(2, 4, 6)).astype(jnp.bfloat16)


def direction_table(angles, wavenumbers, tile_x, tile_y):
    polar_angle = angles[0]
    azimuth = angles[1]
    unit_x = jnp.sin(polar_angle) * jnp.cos(azimuth)
    unit_y = jnp.sin(polar_angle) * jnp.sin(azimuth)
    unit_z = jnp.cos(polar_angle)
    spots = jnp.arange(tile_x * tile_y, dtype=jnp.int32)
    offset_x = (spots // tile_y).astype(jnp.float32)
    offset_y = (spots % tile_y).astype(jnp.float32)
    phase = wavenumbers[:, None, None] * (
        unit_x[None, :, None] * offset_x[None, None, :]
        + unit_y[None, :, None] * offset_y[None, None, :]
    )
    table = jnp.stack([jnp.cos(phase), jnp.sin(phase)]).astype(jnp.bfloat16)
    return (table, (unit_x, unit_y, unit_z))


def far_add(table, units, wavenumbers, pieces, start_x, start_y, start_z):
    grid = jnp.einsum("sfdk,jczk->sfdjcz", table, pieces, preferred_element_type=jnp.float32)
    layers = jnp.arange(pieces.shape[2], dtype=jnp.int32).astype(jnp.float32)
    unit_x, unit_y, unit_z = units
    lateral = unit_x[:, None] * start_x[None, :] + unit_y[:, None] * start_y[None, :]
    height = unit_z[:, None, None] * (start_z[None, :, None] + layers[None, None, :])
    phase = wavenumbers[:, None, None, None] * (lateral[None, :, :, None] + height[None])
    cosine = jnp.cos(phase)[:, :, :, None, :]
    sine = jnp.sin(phase)[:, :, :, None, :]
    real_sum = jnp.sum(grid[0] * cosine - grid[1] * sine, axis=(2, 4))
    imag_sum = jnp.sum(grid[0] * sine + grid[1] * cosine, axis=(2, 4))
    joined = jnp.stack([real_sum, imag_sum])
    return jnp.transpose(joined, (2, 0, 1, 3)).reshape(joined.shape[2], -1)


def shards(fields, material, faces, permittivity, losses, angles, wavenumbers):
    labels = jnp.arange(permittivity.shape[0], dtype=jnp.int32)
    chosen_rows = (material[None] == labels[:, None, None, None]).astype(jnp.float32)
    picked_loss = jnp.sum(chosen_rows * losses[:, None, None, None], axis=0)
    picked_eps = jnp.sum(chosen_rows * permittivity[:, None, None, None], axis=0)
    ratio_keep = (1.0 - picked_loss) / (1.0 + picked_loss)
    ratio_curl = COURANT / (picked_eps * (1.0 + picked_loss))
    state = fields
    for repeat in range(2):
        magnetic = state[3:] - COURANT * curl_forward(state[:3])
        electric = ratio_keep * state[:3] + ratio_curl * curl_backward(magnetic)
        state = jnp.concatenate([electric, magnetic])
    rows = surface_rows(state, faces)
    layers, tile_x, tile_y = (rows.shape[1], rows.shape[2], rows.shape[3])
    local_rows = rows.reshape(1, 12, layers, tile_x * tile_y)
    count_gx = lax.axis_size("gx")
    count_gy = lax.axis_size("gy")
    count_gz = lax.axis_size("gz")
    share_count = DIR_DEV * count_gz
    share = lax.axis_index("gx") * count_gy + lax.axis_index("gy")
    chosen = lax.dynamic_slice_in_dim(angles, share * share_count, share_count, axis=1)
    table, units = direction_table(chosen, wavenumbers, tile_x, tile_y)
    base_z = (lax.axis_index("gz") * layers).astype(jnp.float32)
    piece = lax.all_gather(local_rows, ("gx", "gy"), axis=0, tiled=True)
    order = jnp.arange(piece.shape[0], dtype=jnp.int32)
    start_x = (order // count_gy * tile_x).astype(jnp.float32)
    start_y = (order % count_gy * tile_y).astype(jnp.float32)
    start_z = jnp.zeros((piece.shape[0],), jnp.float32) + base_z
    partial_value = far_add(table, units, wavenumbers, piece, start_x, start_y, start_z)
    summed = lax.psum_scatter(partial_value, "gz", scatter_dimension=0, tiled=True)
    total_cells = layers * count_gz * (tile_x * count_gx) * (tile_y * count_gy)
    scale = 8.0 / math.sqrt(total_cells)
    return (state, summed * scale)


def solution(mesh):
    return jax.shard_map(
        shards,
        mesh=mesh,
        in_specs=(
            P(None, "gz", "gx", "gy"),
            P("gz", "gx", "gy"),
            P(None, "gz", "gx", "gy"),
            P(),
            P(),
            P(),
            P(),
        ),
        out_specs=(P(None, "gz", "gx", "gy"), P(("gx", "gy", "gz"), None)),
        check_vma=False,
    )
```

profile of v0, /device:TPU:0, one launch (start us, length us, event | category | flops | bytes accessed | tf_op | source)
XLA Modules:
  0.0 130.2 jit_solution(8131197896274109318)
XLA Ops:
  8.1 1.3 collective-permute-start
  10.1 1.3 collective-permute-start.1
  12.1 1.3 collective-permute-start.2
  15.5 1.9 %fusion = (bf16[1,4,64,128]{3,2,1,0:T(8,128)(2,1)}, bf16[1,4,64,128]{3,2,1,0:T(8,128)(2,1)}) fusion(f32[64,128]{1,0:T(8,128)S(1)} %multiply_add_fusion, f32[4]{0:T(128)} %param.13), kind=kLoop, calls=%fused_computation.10 | loop fusion | flops 98304 | bytes 163856 | tf_op jit(solution)/shard_map/convert
  17.4 1.4 %multiply_cosine_fusion.1 = (f32[4,64,8]{1,2,0:T(8,128)}, f32[4,64,8]{1,2,0:T(8,128)}) fusion(f32[64,8]{0,1:T(8,128)S(1)} %add_add_fusion, f32[4]{0:T(128)} %param.13), kind=kLoop, calls=%fused_computation.116 | loop fusion | flops 2048 | bytes 18448 | tf_op jit(solution)/shard_map/cos | solution.py:110
  21.0 4.8 %collective-permute-start.3 = (f32[2,4,16,1]{3,2,1,0:T(8,128)S(1)}, f32[2,4,16,1]{3,2,1,0:T(8,128)S(1)}, u32[]{:S(2)}, u32[]{:S(2)}) collective-permute-start(f32[2,4,16,1]{3,2,1,0:T(8,128)S(1)} %pad_maximum_fusion.3), channel_id=1, source_target_pairs={{0,4},{1,5},{2,6},{3,7},{8,12},{9,13},{10,14},{11,15},{16,20},{17,... | collective-permute-start | bytes 1544 | tf_op jit(solution)/shard_map/ppermute | solution.py:17
  25.9 5.3 %collective-permute-start.4 = (f32[2,1,16,128]{3,2,1,0:T(8,128)S(1)}, f32[2,1,16,128]{3,2,1,0:T(8,128)S(1)}, u32[]{:S(2)}, u32[]{:S(2)}) collective-permute-start(f32[2,1,16,128]{3,2,1,0:T(8,128)S(1)} %slice.406), channel_id=1, source_target_pairs={{0,1},{1,2},{2,3},{4,5},{5,6},{6,7},{8,9},{9,10},{10,11},{12,13},{... | collective-permute-start | bytes 49160 | tf_op jit(solution)/shard_map/ppermute | solution.py:17
  31.2 2.5 %collective-permute-start.5 = (f32[2,4,1,128]{3,2,1,0:T(1,128)S(1)}, f32[2,4,1,128]{3,2,1,0:T(1,128)S(1)}, u32[]{:S(2)}, u32[]{:S(2)}) collective-permute-start(f32[2,4,1,128]{3,2,1,0:T(1,128)S(1)} %slice.411), channel_id=1, source_target_pairs={{0,8},{8,16},{16,24},{1,9},{9,17},{17,25},{2,10},{10,18},{18,26},{... | collective-permute-start | bytes 12296 | tf_op jit(solution)/shard_map/ppermute | solution.py:17
  34.7 1.3 collective-permute-start.6
  36.1 1.3 collective-permute-start.7
  37.4 1.3 collective-permute-start.8
  38.7 2.2 %collective-permute-done.6 = f32[2,4,16,1]{3,2,1,0:T(8,128)S(1)} collective-permute-done((f32[2,4,16,1]{3,2,1,0:T(8,128)S(1)}, f32[2,4,16,1]{3,2,1,0:T(8,128)S(1)}, u32[]{:S(2)}, u32[]{:S(2)}) %collective-permute-start.6) | collective-permute-done | bytes 544 | tf_op jit(solution)/shard_map/ppermute | solution.py:17
  40.9 1.2 collective-permute-done.8
  43.6 1.1 stack.99
  45.2 1.1 stack.100
  47.5 4.9 %collective-permute-start.9 = (f32[2,4,16,1]{3,2,1,0:T(8,128)}, f32[2,4,16,1]{3,2,1,0:T(8,128)}, u32[]{:S(2)}, u32[]{:S(2)}) collective-permute-start(f32[2,4,16,1]{3,2,1,0:T(8,128)} %pad_maximum_fusion.1), channel_id=1, source_target_pairs={{0,4},{1,5},{2,6},{3,7},{8,12},{9,13},{10,14},{11,15},{16,20},{17,... | collective-permute-start | bytes 1544 | tf_op jit(solution)/shard_map/ppermute | solution.py:17
  53.0 4.9 %collective-permute-start.10 = (f32[2,1,16,128]{3,2,1,0:T(8,128)}, f32[2,1,16,128]{3,2,1,0:T(8,128)}, u32[]{:S(2)}, u32[]{:S(2)}) collective-permute-start(f32[2,1,16,128]{3,2,1,0:T(8,128)} %slice.440), channel_id=1, source_target_pairs={{0,1},{1,2},{2,3},{4,5},{5,6},{6,7},{8,9},{9,10},{10,11},{12,13},{... | collective-permute-start | bytes 49160 | tf_op jit(solution)/shard_map/ppermute | solution.py:17
  57.8 5.0 %collective-permute-start.11 = (f32[2,4,1,128]{3,2,1,0:T(1,128)S(1)}, f32[2,4,1,128]{3,2,1,0:T(1,128)S(1)}, u32[]{:S(2)}, u32[]{:S(2)}) collective-permute-start(f32[2,4,1,128]{3,2,1,0:T(1,128)S(1)} %slice.445), channel_id=1, source_target_pairs={{0,8},{8,16},{16,24},{1,9},{9,17},{17,25},{2,10},{10,18},{18,26},{... | collective-permute-start | bytes 12296 | tf_op jit(solution)/shard_map/ppermute | solution.py:17
  62.8 1.1 stack.103
  64.4 1.1 stack.104
  65.5 1.1 copy.28
  66.6 1.1 stack.107
  68.1 1.1 stack.108
  72.9 1.1 stack.101
  74.0 1.1 copy.25
  76.2 1.1 copy.26
  78.4 1.1 copy.29
  80.6 1.1 copy.30
  82.8 1.1 copy.33
  85.0 1.1 copy.34
  90.6 11.7 %all_gather.3 = bf16[8,12,1,128]{3,1,2,0:T(8,128)(2,1)S(1)} all-gather(bf16[1,12,1,128]{3,1,2,0:T(8,128)(2,1)S(1)} %convert_element_type.55), channel_id=1, replica_groups=mesh['gx'=4,'gy'=2,'gz'=4] {'gx','gy'}, dimensions={0}, use_global_device_ids=true | all-gather | bytes 27648 | tf_op jit(solution)/shard_map/all_gather | solution.py:141
  104.1 17.7 %reduce-scatter.4.cloned.1.call-done = f32[16,96]{1,0:T(8,128)} async-done(((f32[64,96]{1,0:T(8,128)}), f32[16,96]{1,0:T(8,128)}) %reduce-scatter.4.cloned.1.call-update) | async-done | bytes 6160
  (141 shorter events, 29.1 us)
Async XLA Ops:
  7.2 8.1 %copy-start = (f32[2,512]{1,0:T(2,128)S(1)}, f32[2,512]{1,0:T(2,128)}, u32[]{:S(2)}) copy-start(f32[2,512]{1,0:T(2,128)} %param.12) | copy-start | bytes 12292
  7.2 13.6 %copy-start.1 = (f32[6,4,16,128]{3,2,1,0:T(8,128)S(1)}, f32[6,4,16,128]{3,2,1,0:T(8,128)}, u32[]{:S(2)}) copy-start(f32[6,4,16,128]{3,2,1,0:T(8,128)} %param.7) | copy-start | bytes 589828
  7.2 114.7 %reduce-scatter.4.cloned.1.call-start = ((), (), s32[]{:S(2)}) async-start(), calls=%async_computation.1 | async-start | bytes 40960
  8.1 11.7 %collective-permute-start = (f32[2,4,16,1]{3,2,1,0:T(8,128)S(1)}, f32[2,4,16,1]{3,2,1,0:T(8,128)S(1)}, u32[]{:S(2)}, u32[]{:S(2)}) collective-permute-start(f32[2,4,16,1]{3,2,1,0:T(8,128)S(1)} %pad_maximum_fusion.4), channel_id=1, source_target_pairs={{4,0},{5,1},{6,2},{7,3},{12,8},{13,9},{14,10},{15,11},{20,16},{21,... | collective-permute-start | bytes 1544 | tf_op jit(solution)/shard_map/ppermute | solution.py:17
  10.1 9.7 %collective-permute-start.1 = (f32[2,1,16,128]{3,2,1,0:T(8,128)S(1)}, f32[2,1,16,128]{3,2,1,0:T(8,128)S(1)}, u32[]{:S(2)}, u32[]{:S(2)}) collective-permute-start(f32[2,1,16,128]{3,2,1,0:T(8,128)S(1)} %slice.315), channel_id=1, source_target_pairs={{1,0},{2,1},{3,2},{5,4},{6,5},{7,6},{9,8},{10,9},{11,10},{13,12},{... | collective-permute-start | bytes 49160 | tf_op jit(solution)/shard_map/ppermute | solution.py:17
  12.1 7.6 %collective-permute-start.2 = (f32[2,4,1,128]{3,2,1,0:T(1,128)S(1)}, f32[2,4,1,128]{3,2,1,0:T(1,128)S(1)}, u32[]{:S(2)}, u32[]{:S(2)}) collective-permute-start(f32[2,4,1,128]{3,2,1,0:T(1,128)S(1)} %slice.321), channel_id=1, source_target_pairs={{8,0},{16,8},{24,16},{9,1},{17,9},{25,17},{10,2},{18,10},{26,18},{... | collective-permute-start | bytes 12296 | tf_op jit(solution)/shard_map/ppermute | solution.py:17
  15.3 19.4 %copy-start.7 = (f32[4,16,128]{2,1,0:T(8,128)}, f32[4,16,128]{2,1,0:T(8,128)S(1)}, u32[]{:S(2)}) copy-start(f32[4,16,128]{2,1,0:T(8,128)S(1)} %get-tuple-element.71) | copy-start | bytes 98308
  15.3 19.4 %copy-start.8 = (f32[4,16,128]{2,1,0:T(8,128)}, f32[4,16,128]{2,1,0:T(8,128)S(1)}, u32[]{:S(2)}) copy-start(f32[4,16,128]{2,1,0:T(8,128)S(1)} %get-tuple-element.72) | copy-start | bytes 98308
  21.0 12.7 %collective-permute-start.3 = (f32[2,4,16,1]{3,2,1,0:T(8,128)S(1)}, f32[2,4,16,1]{3,2,1,0:T(8,128)S(1)}, u32[]{:S(2)}, u32[]{:S(2)}) collective-permute-start(f32[2,4,16,1]{3,2,1,0:T(8,128)S(1)} %pad_maximum_fusion.3), channel_id=1, source_target_pairs={{0,4},{1,5},{2,6},{3,7},{8,12},{9,13},{10,14},{11,15},{16,20},{17,... | collective-permute-start | bytes 1544 | tf_op jit(solution)/shard_map/ppermute | solution.py:17
  25.9 8.6 %collective-permute-start.4 = (f32[2,1,16,128]{3,2,1,0:T(8,128)S(1)}, f32[2,1,16,128]{3,2,1,0:T(8,128)S(1)}, u32[]{:S(2)}, u32[]{:S(2)}) collective-permute-start(f32[2,1,16,128]{3,2,1,0:T(8,128)S(1)} %slice.406), channel_id=1, source_target_pairs={{0,1},{1,2},{2,3},{4,5},{5,6},{6,7},{8,9},{9,10},{10,11},{12,13},{... | collective-permute-start | bytes 49160 | tf_op jit(solution)/shard_map/ppermute | solution.py:17
  31.2 3.3 %collective-permute-start.5 = (f32[2,4,1,128]{3,2,1,0:T(1,128)S(1)}, f32[2,4,1,128]{3,2,1,0:T(1,128)S(1)}, u32[]{:S(2)}, u32[]{:S(2)}) collective-permute-start(f32[2,4,1,128]{3,2,1,0:T(1,128)S(1)} %slice.411), channel_id=1, source_target_pairs={{0,8},{8,16},{16,24},{1,9},{9,17},{17,25},{2,10},{10,18},{18,26},{... | collective-permute-start | bytes 12296 | tf_op jit(solution)/shard_map/ppermute | solution.py:17
  34.5 9.1 %copy-start.5 = (f32[1,4,16,128]{3,2,1,0:T(8,128)}, f32[1,4,16,128]{3,2,1,0:T(8,128)S(1)}, u32[]{:S(2)}) copy-start(f32[1,4,16,128]{3,2,1,0:T(8,128)S(1)} %get-tuple-element.53) | copy-start | bytes 98308
  34.6 9.0 %copy-start.6 = (f32[1,4,16,128]{3,2,1,0:T(8,128)}, f32[1,4,16,128]{3,2,1,0:T(8,128)S(1)}, u32[]{:S(2)}) copy-start(f32[1,4,16,128]{3,2,1,0:T(8,128)S(1)} %fusion.14) | copy-start | bytes 98308
  34.7 6.2 %collective-permute-start.6 = (f32[2,4,16,1]{3,2,1,0:T(8,128)S(1)}, f32[2,4,16,1]{3,2,1,0:T(8,128)S(1)}, u32[]{:S(2)}, u32[]{:S(2)}) collective-permute-start(f32[2,4,16,1]{3,2,1,0:T(8,128)S(1)} %pad_maximum_fusion.2), channel_id=1, source_target_pairs={{4,0},{5,1},{6,2},{7,3},{12,8},{13,9},{14,10},{15,11},{20,16},{21,... | collective-permute-start | bytes 1544 | tf_op jit(solution)/shard_map/ppermute | solution.py:17
  36.1 5.9 %collective-permute-start.7 = (f32[2,1,16,128]{3,2,1,0:T(8,128)S(1)}, f32[2,1,16,128]{3,2,1,0:T(8,128)S(1)}, u32[]{:S(2)}, u32[]{:S(2)}) collective-permute-start(f32[2,1,16,128]{3,2,1,0:T(8,128)S(1)} %slice.423), channel_id=1, source_target_pairs={{1,0},{2,1},{3,2},{5,4},{6,5},{7,6},{9,8},{10,9},{11,10},{13,12},{... | collective-permute-start | bytes 49160 | tf_op jit(solution)/shard_map/ppermute | solution.py:17
  37.4 4.6 %collective-permute-start.8 = (f32[2,4,1,128]{3,2,1,0:T(1,128)S(1)}, f32[2,4,1,128]{3,2,1,0:T(1,128)S(1)}, u32[]{:S(2)}, u32[]{:S(2)}) collective-permute-start(f32[2,4,1,128]{3,2,1,0:T(1,128)S(1)} %slice.429), channel_id=1, source_target_pairs={{8,0},{16,8},{24,16},{9,1},{17,9},{25,17},{10,2},{18,10},{26,18},{... | collective-permute-start | bytes 12296 | tf_op jit(solution)/shard_map/ppermute | solution.py:17
  47.5 22.2 %collective-permute-start.9 = (f32[2,4,16,1]{3,2,1,0:T(8,128)}, f32[2,4,16,1]{3,2,1,0:T(8,128)}, u32[]{:S(2)}, u32[]{:S(2)}) collective-permute-start(f32[2,4,16,1]{3,2,1,0:T(8,128)} %pad_maximum_fusion.1), channel_id=1, source_target_pairs={{0,4},{1,5},{2,6},{3,7},{8,12},{9,13},{10,14},{11,15},{16,20},{17,... | collective-permute-start | bytes 1544 | tf_op jit(solution)/shard_map/ppermute | solution.py:17
  53.0 17.5 %collective-permute-start.10 = (f32[2,1,16,128]{3,2,1,0:T(8,128)}, f32[2,1,16,128]{3,2,1,0:T(8,128)}, u32[]{:S(2)}, u32[]{:S(2)}) collective-permute-start(f32[2,1,16,128]{3,2,1,0:T(8,128)} %slice.440), channel_id=1, source_target_pairs={{0,1},{1,2},{2,3},{4,5},{5,6},{6,7},{8,9},{9,10},{10,11},{12,13},{... | collective-permute-start | bytes 49160 | tf_op jit(solution)/shard_map/ppermute | solution.py:17
  57.8 12.6 %collective-permute-start.11 = (f32[2,4,1,128]{3,2,1,0:T(1,128)S(1)}, f32[2,4,1,128]{3,2,1,0:T(1,128)S(1)}, u32[]{:S(2)}, u32[]{:S(2)}) collective-permute-start(f32[2,4,1,128]{3,2,1,0:T(1,128)S(1)} %slice.445), channel_id=1, source_target_pairs={{0,8},{8,16},{16,24},{1,9},{9,17},{17,25},{2,10},{10,18},{18,26},{... | collective-permute-start | bytes 12296 | tf_op jit(solution)/shard_map/ppermute | solution.py:17
  67.7 3.6 %copy-start.11 = (f32[1,4,16,127]{3,2,1,0:T(8,128)S(1)}, f32[1,4,16,127]{3,2,1,0:T(8,128)}, u32[]{:S(2)}) copy-start(f32[1,4,16,127]{3,2,1,0:T(8,128)} %get-tuple-element.94) | copy-start | bytes 97540
  83.9 4.1 %copy-start.2 = (f32[1,1,4,4,4,32,4]{5,6,4,3,2,1,0:T(4,128)S(1)}, f32[1,1,4,4,4,32,4]{5,6,4,3,2,1,0:T(4,128)}, u32[]{:S(2)}) copy-start(f32[1,1,4,4,4,32,4]{5,6,4,3,2,1,0:T(4,128)} %copy.28) | copy-start | bytes 98308
  86.1 3.9 %copy-start.3 = (f32[1,1,4,4,4,32,4]{5,6,4,3,2,1,0:T(4,128)S(1)}, f32[1,1,4,4,4,32,4]{5,6,4,3,2,1,0:T(4,128)}, u32[]{:S(2)}) copy-start(f32[1,1,4,4,4,32,4]{5,6,4,3,2,1,0:T(4,128)} %copy.33) | copy-start | bytes 98308
  86.1 4.0 %copy-start.4 = (f32[1,1,4,4,4,32,4]{5,6,4,3,2,1,0:T(4,128)S(1)}, f32[1,1,4,4,4,32,4]{5,6,4,3,2,1,0:T(4,128)}, u32[]{:S(2)}) copy-start(f32[1,1,4,4,4,32,4]{5,6,4,3,2,1,0:T(4,128)} %copy.34) | copy-start | bytes 98308
  88.1 14.2 %copy-start.9 = (bf16[1,4,64,128]{3,2,1,0:T(8,128)(2,1)S(1)}, bf16[1,4,64,128]{3,2,1,0:T(8,128)(2,1)}, u32[]{:S(2)}) copy-start(bf16[1,4,64,128]{3,2,1,0:T(8,128)(2,1)} %get-tuple-element.69) | copy-start | bytes 196612
  88.1 14.2 %copy-start.10 = (bf16[1,4,64,128]{3,2,1,0:T(8,128)(2,1)S(1)}, bf16[1,4,64,128]{3,2,1,0:T(8,128)(2,1)}, u32[]{:S(2)}) copy-start(bf16[1,4,64,128]{3,2,1,0:T(8,128)(2,1)} %get-tuple-element.70) | copy-start | bytes 196612
  90.0 12.6 %copy-start.12 = (f32[4,64,8]{1,2,0:T(8,128)S(1)}, f32[4,64,8]{1,2,0:T(8,128)}, u32[]{:S(2)}) copy-start(f32[4,64,8]{1,2,0:T(8,128)} %get-tuple-element.81) | copy-start | bytes 24580
  90.0 12.6 %copy-start.13 = (f32[4,64,8]{1,2,0:T(8,128)S(1)}, f32[4,64,8]{1,2,0:T(8,128)}, u32[]{:S(2)}) copy-start(f32[4,64,8]{1,2,0:T(8,128)} %get-tuple-element.82) | copy-start | bytes 24580
Sparse Core Ops, SparseCore 0:
  103.6 18.2 reduce-scatter.3
where the time goes:
time: 131 us; the launch traced here: 130 us
  local copies, waits for them, and re-layouts  36.1 us (28%)
  starting transfers between devices  35.1 us (27%)
  waiting for transfers between devices  21.9 us (17%)
  between operations  14.8 us (11%)
  blocking collectives  11.7 us (9%)
  other arithmetic  10.5 us (8%)
    ppermute x12, starting transfers between devices, passed_along(): return lax.ppermute(shard, axis, pairs)  35 us
    another operation x25, local copies, waits for them, and re-layouts, surface_rows(): jnp.stack([-state[5] * normal_x, state[4] * normal_x, state[2] * normal_x...  22.9 us
    unnamed x2, waiting for transfers between devices  17.7 us
    all_gather x1, blocking collectives, shards(): piece = lax.all_gather(local_rows, ('gx', 'gy'), axis=0, tiled=True)  11.7 us
    unnamed x42, local copies, waits for them, and re-layouts  6.12 us
    ppermute x12, waiting for transfers between devices, passed_along(): return lax.ppermute(shard, axis, pairs)  4.13 us
  transfers between devices with their start and end apart: 13, of which 4 were waited for; matrix products, arithmetic and copies ran while one was open for 13% of the time, Pallas kernels for 0%

commit v1 on v0

v1 whole, which is shorter than its diff:
```python
import functools
import math

import jax
import jax.numpy as jnp
from jax import lax
from jax.experimental import pallas as pl
from jax.experimental.pallas import tpu as pltpu
from jax.sharding import PartitionSpec as P

MESH = pl.DeviceIdType.MESH
COURANT = 0.5
BLOCK = 4
CHANNELS = 12
ROWS = 16
AXES = ("gz", "gx", "gy")


def iota(shape, axis):
    return lax.broadcasted_iota(jnp.int32, shape, axis)


def split_dot(left, right):
    high = left.astype(jnp.bfloat16)
    low = (left - high.astype(jnp.float32)).astype(jnp.bfloat16)
    return jnp.dot(high, right, preferred_element_type=jnp.float32) + jnp.dot(
        low, right, preferred_element_type=jnp.float32
    )


def kernel(
    counts,
    dirs,
    fields_ref,
    material_ref,
    faces_ref,
    eps_ref,
    loss_ref,
    angles_ref,
    wave_ref,
    state_ref,
    far_ref,
    send_x,
    send_y,
    halo_z,
    halo_x,
    halo_y,
    gathered,
    send_sem,
    recv_sem,
    rows_send_sem,
    rows_recv_sem,
):
    n_gz, n_gx, n_gy = counts
    total = n_gz * n_gx * n_gy
    place = {axis: lax.axis_index(axis) for axis in AXES}
    at_z, at_x, at_y = (place[axis] for axis in AXES)
    me = (at_z * n_gx + at_x) * n_gy + at_y

    def coords(number):
        return {
            "gz": number // (n_gx * n_gy),
            "gx": (number // n_gy) % n_gx,
            "gy": number % n_gy,
        }

    barrier = pltpu.get_barrier_semaphore()

    def greet(step, carry):
        pl.semaphore_signal(
            barrier, inc=1, device_id=coords((me + step) % total), device_id_type=MESH
        )
        return carry

    lax.fori_loop(1, total, greet, 0)

    depth, width, height = fields_ref.shape[1:]
    plane = (width, height)
    lane = iota(plane, 1)
    row = iota(plane, 0)

    material = material_ref[...]
    loss = jnp.zeros(material.shape, jnp.float32)
    eps = jnp.zeros(material.shape, jnp.float32)
    for label in range(eps_ref.shape[0]):
        chosen = material == label
        loss = jnp.where(chosen, loss_ref[label], loss)
        eps = jnp.where(chosen, eps_ref[label], eps)
    keep = (1.0 - loss) / (1.0 + loss)
    gain = COURANT / (eps * (1.0 + loss))

    pl.semaphore_wait(barrier, total - 1)

    def exchange(stage, source, base, comps_x, comps_y, edge_z, edge_x, edge_y, by):
        for at, comp in enumerate(comps_x):
            for z in range(depth):
                k = at * depth + z
                send_x[stage, k : k + 1, :] = source[base + comp, z, edge_x : edge_x + 1, :]
        packed = jnp.zeros(plane, jnp.float32)
        for at, comp in enumerate(comps_y):
            for z in range(depth):
                column = source[base + comp, z, :, edge_y : edge_y + 1]
                packed = jnp.where(
                    lane == at * depth + z, jnp.broadcast_to(column, plane), packed
                )
        send_y[stage] = packed
        sources = (
            source.at[pl.ds(base, 2), edge_z],
            send_x.at[stage],
            send_y.at[stage],
        )
        targets = (halo_z.at[stage], halo_x.at[stage], halo_y.at[stage])
        copies = []
        for way, axis in enumerate(AXES):
            last = counts[way] - 1
            copies.append(
                pltpu.make_async_remote_copy(
                    src_ref=sources[way],
                    dst_ref=targets[way],
                    send_sem=send_sem.at[stage, way],
                    recv_sem=recv_sem.at[stage, way],
                    device_id={axis: place[axis] + by},
                    device_id_type=MESH,
                )
            )
            sends = place[axis] > 0 if by < 0 else place[axis] < last

            @pl.when(sends)
            def _():
                copies[way].start()

        return copies

    def land(copies, stage, by):
        halos = (halo_z, halo_x, halo_y)
        for way, axis in enumerate(AXES):
            last = counts[way] - 1
            sends = place[axis] > 0 if by < 0 else place[axis] < last
            takes = place[axis] < last if by < 0 else place[axis] > 0

            @pl.when(sends)
            def _():
                copies[way].wait_send()

            @pl.when(takes)
            def _():
                copies[way].wait_recv()

            @pl.when(jnp.logical_not(takes))
            def _():
                halos[way][stage] = jnp.zeros(halos[way].shape[1:], jnp.float32)

    def next_z(field, stage, at):
        return [field[z] for z in range(1, depth)] + [halo_z[stage, at]]

    def prev_z(field, stage, at):
        return [halo_z[stage, at]] + [field[z] for z in range(depth - 1)]

    def next_x(field, stage, at):
        out = []
        for z in range(depth):
            k = at * depth + z
            edge = jnp.broadcast_to(halo_x[stage, k : k + 1, :], plane)
            out.append(jnp.where(row == width - 1, edge, pltpu.roll(field[z], width - 1, 0)))
        return out

    def prev_x(field, stage, at):
        out = []
        for z in range(depth):
            k = at * depth + z
            edge = jnp.broadcast_to(halo_x[stage, k : k + 1, :], plane)
            out.append(jnp.where(row == 0, edge, pltpu.roll(field[z], 1, 0)))
        return out

    def next_y(field, stage, at):
        out = []
        for z in range(depth):
            k = at * depth + z
            edge = jnp.broadcast_to(halo_y[stage, :, k : k + 1], plane)
            out.append(jnp.where(lane == height - 1, edge, pltpu.roll(field[z], height - 1, 1)))
        return out

    def prev_y(field, stage, at):
        out = []
        for z in range(depth):
            k = at * depth + z
            edge = jnp.broadcast_to(halo_y[stage, :, k : k + 1], plane)
            out.append(jnp.where(lane == 0, edge, pltpu.roll(field[z], 1, 1)))
        return out

    def magnetic_step(source, stage):
        ex, ey, ez = ([source[c, z] for z in range(depth)] for c in range(3))
        ey_z, ex_z = next_z(ey, stage, 1), next_z(ex, stage, 0)
        ey_x, ez_x = next_x(ey, stage, 0), next_x(ez, stage, 1)
        ex_y, ez_y = next_y(ex, stage, 0), next_y(ez, stage, 1)
        for z in range(depth):
            curl = (
                (ez_y[z] - ez[z]) - (ey_z[z] - ey[z]),
                (ex_z[z] - ex[z]) - (ez_x[z] - ez[z]),
                (ey_x[z] - ey[z]) - (ex_y[z] - ex[z]),
            )
            for c in range(3):
                state_ref[3 + c, z] = source[3 + c, z] - COURANT * curl[c]

    def electric_step(source, stage):
        hx, hy, hz = ([state_ref[3 + c, z] for z in range(depth)] for c in range(3))
        hy_z, hx_z = prev_z(hy, stage, 1), prev_z(hx, stage, 0)
        hy_x, hz_x = prev_x(hy, stage, 0), prev_x(hz, stage, 1)
        hx_y, hz_y = prev_y(hx, stage, 0), prev_y(hz, stage, 1)
        for z in range(depth):
            curl = (
                (hz[z] - hz_y[z]) - (hy[z] - hy_z[z]),
                (hx[z] - hx_z[z]) - (hz[z] - hz_x[z]),
                (hy[z] - hy_x[z]) - (hx[z] - hx_y[z]),
            )
            for c in range(3):
                state_ref[c, z] = keep[z] * source[c, z] + gain[z] * curl[c]

    tile_x, tile_y = width // BLOCK, height // BLOCK
    spots = tile_x * tile_y
    freqs = wave_ref.shape[0]
    columns = 2 * freqs * dirs

    def steering():
        spot = iota((1, columns), 1)
        spot_d = spot % dirs
        spot_f = (spot // dirs) % freqs
        base = ((at_x * n_gy + at_y) * n_gz + at_z) * dirs
        polar = jnp.zeros((1, columns), jnp.float32)
        azimuth = jnp.zeros((1, columns), jnp.float32)
        wave = jnp.zeros((1, columns), jnp.float32)
        for d in range(dirs):
            polar = jnp.where(spot_d == d, angles_ref[0, base + d], polar)
            azimuth = jnp.where(spot_d == d, angles_ref[1, base + d], azimuth)
        for f in range(freqs):
            wave = jnp.where(spot_f == f, wave_ref[f], wave)
        unit_x = jnp.sin(polar) * jnp.cos(azimuth)
        unit_y = jnp.sin(polar) * jnp.sin(azimuth)
        unit_z = jnp.cos(polar)
        return wave, unit_x, unit_y, unit_z, spot

    def offset_table(steer):
        wave, unit_x, unit_y, unit_z, spot = steer
        cell = iota((spots, columns), 0)
        offset_x = (cell // tile_y).astype(jnp.float32)
        offset_y = (cell % tile_y).astype(jnp.float32)
        phase = wave * (unit_x * offset_x + unit_y * offset_y)
        quarter = jnp.where(spot >= columns // 2, math.pi / 2, 0.0)
        return jnp.cos(phase - quarter).astype(jnp.bfloat16)

    def tile_phases(steer):
        wave, unit_x, unit_y, unit_z, spot = steer
        tile = iota((total, columns), 0)
        start_z = (tile // (n_gx * n_gy)).astype(jnp.float32)
        start_x = ((tile // n_gy) % n_gx * tile_x).astype(jnp.float32)
        start_y = (tile % n_gy * tile_y).astype(jnp.float32)
        phase = wave * (unit_x * start_x + unit_y * start_y + unit_z * start_z)
        return jnp.cos(phase), jnp.sin(phase)

    copies = exchange(0, fields_ref, 0, (1, 2), (0, 2), 0, 0, 0, -1)
    steer = steering()
    land(copies, 0, -1)
    magnetic_step(fields_ref, 0)
    copies = exchange(1, state_ref, 3, (1, 2), (0, 2), depth - 1, width - 1, height - 1, 1)
    table = offset_table(steer)
    land(copies, 1, 1)
    electric_step(fields_ref, 1)
    copies = exchange(2, state_ref, 0, (1, 2), (0, 2), 0, 0, 0, -1)
    turn_cos, turn_sin = tile_phases(steer)
    land(copies, 2, -1)
    magnetic_step(state_ref, 2)
    copies = exchange(3, state_ref, 3, (1, 2), (0, 2), depth - 1, width - 1, height - 1, 1)
    masks = faces_ref[...].astype(jnp.float32)
    land(copies, 3, 1)
    electric_step(state_ref, 3)

    parts = (
        (5, 0, -1.0), (4, 0, 1.0), (2, 0, 1.0), (1, 0, -1.0),
        (5, 1, 1.0), (3, 1, -1.0), (2, 1, -1.0), (0, 1, 1.0),
        (4, 2, -1.0), (3, 2, 1.0), (1, 2, 1.0), (0, 2, -1.0),
    )
    sums = []
    for comp, normal, sign in parts:
        one = state_ref[comp, 0] * masks[normal, 0]
        for z in range(1, depth):
            one = one + state_ref[comp, z] * masks[normal, z]
        sums.append(one * (sign / BLOCK**3))
    stacked = jnp.concatenate(sums, axis=0)
    take = (iota((height, spots), 1) % tile_y == iota((height, spots), 0) // BLOCK)
    spread = split_dot(stacked, take.astype(jnp.float32).astype(jnp.bfloat16))
    own = iota((width, spots), 1) // tile_y == iota((width, spots), 0) // BLOCK
    own_rows = [
        jnp.sum(
            jnp.where(own, spread[c * width : (c + 1) * width], 0.0), axis=0, keepdims=True
        )
        for c in range(CHANNELS)
    ]
    own_rows.append(jnp.zeros((ROWS - CHANNELS, spots), jnp.float32))
    gathered[me] = jnp.concatenate(own_rows, axis=0).astype(jnp.bfloat16)

    def rows_copy(slot, other):
        return pltpu.make_async_remote_copy(
            src_ref=gathered.at[slot],
            dst_ref=gathered.at[slot],
            send_sem=rows_send_sem.at[other],
            recv_sem=rows_recv_sem.at[slot],
            device_id=coords(other),
            device_id_type=MESH,
        )

    def send_rows(step, carry):
        rows_copy(me, (me + step) % total).start()
        return carry

    def take_rows(step, carry):
        other = (me + step) % total
        rows_copy(other, other).wait_recv()
        rows_copy(me, other).wait_send()
        return carry

    lax.fori_loop(1, total, send_rows, 0)
    lax.fori_loop(1, total, take_rows, 0)

    grid = jnp.dot(
        gathered[...].reshape(total * ROWS, spots), table, preferred_element_type=jnp.float32
    ).reshape(total, ROWS, columns)
    by_cos = jnp.sum(grid * turn_cos[:, None, :], axis=0)
    by_sin = jnp.sum(grid * turn_sin[:, None, :], axis=0)
    half = columns // 2
    crossed = pltpu.roll(by_sin, half, 1)
    column = iota((ROWS, columns), 1)
    joined = jnp.where(column < half, by_cos - crossed, by_cos + crossed)
    scale = 8.0 / math.sqrt(total * spots)
    turned = jnp.transpose(joined * scale)
    for k in range(2 * freqs):
        far_ref[:, k * CHANNELS : (k + 1) * CHANNELS] = turned[k * dirs : (k + 1) * dirs, :CHANNELS]


def shards(counts, fields, material, faces, permittivity, losses, angles, wavenumbers):
    total = math.prod(counts)
    depth, width, height = fields.shape[1:]
    dirs = angles.shape[1] // total
    freqs = wavenumbers.shape[0]
    spots = (width // BLOCK) * (height // BLOCK)
    vmem = pl.BlockSpec(memory_space=pltpu.VMEM)
    smem = pl.BlockSpec(memory_space=pltpu.SMEM)
    return pl.pallas_call(
        functools.partial(kernel, counts, dirs),
        out_shape=(
            jax.ShapeDtypeStruct(fields.shape, jnp.float32),
            jax.ShapeDtypeStruct((dirs, 2 * freqs * CHANNELS), jnp.float32),
        ),
        in_specs=[vmem, vmem, vmem, smem, smem, smem, smem],
        out_specs=(vmem, vmem),
        scratch_shapes=[
            pltpu.VMEM((4, 2 * depth, height), jnp.float32),
            pltpu.VMEM((4, width, height), jnp.float32),
            pltpu.VMEM((4, 2, width, height), jnp.float32),
            pltpu.VMEM((4, 2 * depth, height), jnp.float32),
            pltpu.VMEM((4, width, height), jnp.float32),
            pltpu.VMEM((total, ROWS, spots), jnp.bfloat16),
            pltpu.SemaphoreType.DMA((4, 3)),
            pltpu.SemaphoreType.DMA((4, 3)),
            pltpu.SemaphoreType.DMA((total,)),
            pltpu.SemaphoreType.DMA((total,)),
        ],
        compiler_params=pltpu.CompilerParams(
            collective_id=0, has_side_effects=True, vmem_limit_bytes=48 * 1024 * 1024
        ),
    )(fields, material, faces, permittivity, losses, angles, wavenumbers)


def solution(mesh):
    counts = tuple(mesh.shape[axis] for axis in AXES)
    return jax.shard_map(
        functools.partial(shards, counts),
        mesh=mesh,
        in_specs=(
            P(None, "gz", "gx", "gy"),
            P("gz", "gx", "gy"),
            P(None, "gz", "gx", "gy"),
            P(),
            P(),
            P(),
            P(),
        ),
        out_specs=(P(None, "gz", "gx", "gy"), P(("gx", "gy", "gz"), None)),
        check_vma=False,
    )
```

time: 131 us -> 32.1 us (0.25)
  starting transfers between devices: 35.1 us -> 0 us
  local copies, waits for them, and re-layouts: 36.1 us -> 6.5 us
  Pallas kernels: 0 us -> 24.6 us
  waiting for transfers between devices: 21.9 us -> 0 us
  between operations: 14.8 us -> 0.66 us
  blocking collectives: 11.7 us -> 0 us
  other arithmetic: 10.5 us -> 0 us
    ppermute x12 -> x0, starting transfers between devices: 35 us -> none  [passed_along(): return lax.ppermute(shard, axis, pairs)]
    pallas_call x0 -> x1, Pallas kernels: none -> 24.6 us  [shards(): pl.pallas_call(functools.partial(kernel, counts, dirs), out_shape=(jax.Sh...]
    another operation x25 -> x0, local copies, waits for them, and re-layouts: 22.9 us -> none  [surface_rows(): jnp.stack([-state[5] * normal_x, state[4] * normal_x, state[2] * normal_x...]
    unnamed x2 -> x0, waiting for transfers between devices: 17.7 us -> none
    all_gather x1 -> x0, blocking collectives: 11.7 us -> none  [shards(): piece = lax.all_gather(local_rows, ('gx', 'gy'), axis=0, tiled=True)]
    slice x24 -> x0, local copies, waits for them, and re-layouts: 5.05 us -> none  [the longest x2 0.8 us: curl_backward(): prev_y[1]]
    ppermute x12 -> x0, waiting for transfers between devices: 4.13 us -> none  [passed_along(): return lax.ppermute(shard, axis, pairs)]
    another operation x5 -> x0, other arithmetic: 2.67 us -> none
  transfers between devices with their start and end apart: 13 -> 0, of which waited for: 4 -> 0; matrix products, arithmetic and copies ran while one was open for 13% -> 0% of each run, Pallas kernels for 0% -> 0%
where the time goes in v1:
time: 32.1 us; the launch traced here: 31.8 us
  Pallas kernels  24.6 us (77%)
  local copies, waits for them, and re-layouts  6.5 us (20%)
  between operations  0.66 us (2%)
    pallas_call x1, Pallas kernels, shards(): pl.pallas_call(functools.partial(kernel, counts, dirs), out_shape=(jax.Sh...  24.6 us
    unnamed x16, local copies, waits for them, and re-layouts  6.5 us

profile of v1, /device:TPU:0, one launch (start us, length us, event | category | flops | bytes accessed | tf_op | source)
XLA Modules:
  0.0 31.8 jit_solution(4166580352275093519)
XLA Ops:
  0.6 0.0 copy-start
  0.6 0.9 %copy-done = f32[6,4,16,128]{3,2,1,0:T(8,128)S(1)} copy-done((f32[6,4,16,128]{3,2,1,0:T(8,128)S(1)}, f32[6,4,16,128]{3,2,1,0:T(8,128)}, u32[]{:S(2)}) %copy-start) | copy-done | bytes 196632
  1.6 0.0 copy-start.1
  1.6 0.9 %copy-done.1 = s32[3,4,16,128]{3,2,1,0:T(8,128)S(1)} copy-done((s32[3,4,16,128]{3,2,1,0:T(8,128)S(1)}, s32[3,4,16,128]{3,2,1,0:T(8,128)}, u32[]{:S(2)}) %copy-start.1) | copy-done | bytes 98328
  2.5 0.0 copy-start.2
  2.5 0.8 %copy-done.2 = s32[4,16,128]{2,1,0:T(8,128)S(1)} copy-done((s32[4,16,128]{2,1,0:T(8,128)S(1)}, s32[4,16,128]{2,1,0:T(8,128)}, u32[]{:S(2)}) %copy-start.2) | copy-done | bytes 32792
  3.2 0.0 copy-start.3
  3.2 0.7 %copy-done.3 = f32[2,512]{1,0:T(2,128)S(1)} copy-done((f32[2,512]{1,0:T(2,128)S(1)}, f32[2,512]{1,0:T(2,128)}, u32[]{:S(2)}) %copy-start.3) | copy-done | bytes 4120
  3.9 0.0 copy-start.4
  3.9 0.7 %copy-done.4 = f32[16]{0:T(128)S(1)} copy-done((f32[16]{0:T(128)S(1)}, f32[16]{0:T(128)}, u32[]{:S(2)}) %copy-start.4) | copy-done | bytes 88
  4.6 0.0 copy-start.5
  4.6 0.7 %copy-done.5 = f32[16]{0:T(128)S(1)} copy-done((f32[16]{0:T(128)S(1)}, f32[16]{0:T(128)}, u32[]{:S(2)}) %copy-start.5) | copy-done | bytes 88
  5.2 0.0 copy-start.6
  5.2 0.7 %copy-done.6 = f32[4]{0:T(128)S(1)} copy-done((f32[4]{0:T(128)S(1)}, f32[4]{0:T(128)}, u32[]{:S(2)}) %copy-start.6) | copy-done | bytes 40
  5.9 24.6 %shard_map.86 = (f32[6,4,16,128]{3,2,1,0:T(8,128)S(1)}, f32[16,96]{1,0:T(8,128)S(1)}) custom-call(f32[6,4,16,128]{3,2,1,0:T(8,128)S(1)} %copy-done, s32[4,16,128]{2,1,0:T(8,128)S(1)} %copy-done.2, s32[3,4,16,128]{3,2,1,0:T(8,128)S(1)} %copy-done.1, f32[16]{0:T(128)S(1)} %copy-done.4, f32[16]{0:T(128)S(1)} %copy-done.5, f32[2,512]{1,0:T(2,128)S(1)} %copy-done.3, ...), custom_call_target="tpu_custom_call" | custom-call | tf_op jit(solution)/shard_map/pallas_call | solution.py:347
  30.5 0.7 %copy.11 = f32[6,4,16,128]{3,2,1,0:T(8,128)} copy(f32[6,4,16,128]{3,2,1,0:T(8,128)S(1)} %get-tuple-element.4) | data formatting | bytes 393216
  31.2 0.6 %copy.12 = f32[16,96]{1,0:T(8,128)} copy(f32[16,96]{1,0:T(8,128)S(1)} %get-tuple-element.5) | data formatting | bytes 12288
Async XLA Ops:
  0.6 0.9 %copy-start = (f32[6,4,16,128]{3,2,1,0:T(8,128)S(1)}, f32[6,4,16,128]{3,2,1,0:T(8,128)}, u32[]{:S(2)}) copy-start(f32[6,4,16,128]{3,2,1,0:T(8,128)} %fields_ref.1) | copy-start | bytes 589828
  1.6 0.9 %copy-start.1 = (s32[3,4,16,128]{3,2,1,0:T(8,128)S(1)}, s32[3,4,16,128]{3,2,1,0:T(8,128)}, u32[]{:S(2)}) copy-start(s32[3,4,16,128]{3,2,1,0:T(8,128)} %faces_ref.1) | copy-start | bytes 294916
  2.5 0.8 %copy-start.2 = (s32[4,16,128]{2,1,0:T(8,128)S(1)}, s32[4,16,128]{2,1,0:T(8,128)}, u32[]{:S(2)}) copy-start(s32[4,16,128]{2,1,0:T(8,128)} %material_ref.1) | copy-start | bytes 98308
  3.2 0.7 %copy-start.3 = (f32[2,512]{1,0:T(2,128)S(1)}, f32[2,512]{1,0:T(2,128)}, u32[]{:S(2)}) copy-start(f32[2,512]{1,0:T(2,128)} %angles_ref.1) | copy-start | bytes 12292
  3.9 0.7 %copy-start.4 = (f32[16]{0:T(128)S(1)}, f32[16]{0:T(128)}, u32[]{:S(2)}) copy-start(f32[16]{0:T(128)} %eps_ref.1) | copy-start | bytes 196
  4.6 0.7 %copy-start.5 = (f32[16]{0:T(128)S(1)}, f32[16]{0:T(128)}, u32[]{:S(2)}) copy-start(f32[16]{0:T(128)} %loss_ref.1) | copy-start | bytes 196
  5.2 0.7 %copy-start.6 = (f32[4]{0:T(128)S(1)}, f32[4]{0:T(128)}, u32[]{:S(2)}) copy-start(f32[4]{0:T(128)} %wave_ref.1) | copy-start | bytes 52

commit v2 on v1

v2 whole, which is shorter than its diff:
```python
import functools
import math

import jax
import jax.numpy as jnp
from jax import lax
from jax.experimental import pallas as pl
from jax.experimental.pallas import tpu as pltpu
from jax.sharding import PartitionSpec as P

MESH = pl.DeviceIdType.MESH
COURANT = 0.5
BLOCK = 4
CHANNELS = 12
ROWS = 16
AXES = ("gz", "gx", "gy")


def iota(shape, axis):
    return lax.broadcasted_iota(jnp.int32, shape, axis)


def split_dot(left, right):
    high = left.astype(jnp.bfloat16)
    low = (left - high.astype(jnp.float32)).astype(jnp.bfloat16)
    return jnp.dot(high, right, preferred_element_type=jnp.float32) + jnp.dot(
        low, right, preferred_element_type=jnp.float32
    )


def kernel(
    counts,
    dirs,
    fields_hbm,
    material_hbm,
    faces_hbm,
    eps_hbm,
    loss_hbm,
    angles_hbm,
    wave_hbm,
    state_ref,
    far_ref,
    fields_ref,
    material_ref,
    faces_ref,
    eps_ref,
    loss_ref,
    angles_ref,
    wave_ref,
    send_x,
    send_y,
    halo_z,
    halo_x,
    halo_y,
    edge_zy,
    edge_zx,
    edge_xz,
    edge_xy,
    edge_yz,
    edge_yx,
    gathered,
    local_sem,
    send_sem,
    recv_sem,
    rows_send_sem,
    rows_recv_sem,
):
    n_gz, n_gx, n_gy = counts
    total = n_gz * n_gx * n_gy
    place = {axis: lax.axis_index(axis) for axis in AXES}
    at_z, at_x, at_y = (place[axis] for axis in AXES)
    me = (at_z * n_gx + at_x) * n_gy + at_y

    def coords(number):
        return {
            "gz": number // (n_gx * n_gy),
            "gx": (number // n_gy) % n_gx,
            "gy": number % n_gy,
        }

    pairs = (
        (fields_hbm, fields_ref),
        (material_hbm, material_ref),
        (loss_hbm, loss_ref),
        (eps_hbm, eps_ref),
        (angles_hbm, angles_ref),
        (wave_hbm, wave_ref),
        (faces_hbm, faces_ref),
    )
    loads = [pltpu.make_async_copy(a, b, local_sem.at[k]) for k, (a, b) in enumerate(pairs)]
    for load in loads:
        load.start()

    barrier = pltpu.get_barrier_semaphore()

    def greet(step, carry):
        pl.semaphore_signal(
            barrier, inc=1, device_id=coords((me + step) % total), device_id_type=MESH
        )
        return carry

    lax.fori_loop(1, total, greet, 0)

    depth, width, height = fields_ref.shape[1:]
    plane = (width, height)
    lane = iota(plane, 1)
    row = iota(plane, 0)
    levels = range(depth)

    def later_x(field):
        return [jnp.where(row == width - 1, 0.0, pltpu.roll(f, width - 1, 0)) for f in field]

    def later_y(field):
        return [jnp.where(lane == height - 1, 0.0, pltpu.roll(f, height - 1, 1)) for f in field]

    def magnetic_inside(source):
        ex, ey, ez = ([source[c, z] for z in levels] for c in range(3))
        none = jnp.zeros(plane, jnp.float32)
        ey_z, ex_z = ey[1:] + [none], ex[1:] + [none]
        ey_x, ez_x = later_x(ey), later_x(ez)
        ex_y, ez_y = later_y(ex), later_y(ez)
        for z in levels:
            curl = (
                (ez_y[z] - ez[z]) - (ey_z[z] - ey[z]),
                (ex_z[z] - ex[z]) - (ez_x[z] - ez[z]),
                (ey_x[z] - ey[z]) - (ex_y[z] - ex[z]),
            )
            for c in range(3):
                state_ref[3 + c, z] = source[3 + c, z] - COURANT * curl[c]

    def pack_faces(source, stage):
        for side, ref, base, edge_x, edge_y in (
            (0, source, 0, 0, 0),
            (1, state_ref, 3, width - 1, height - 1),
        ):
            for at, comp in enumerate((1, 2)):
                for z in levels:
                    k = at * depth + z
                    send_x[stage, side, k : k + 1, :] = ref[base + comp, z, edge_x : edge_x + 1, :]
            packed = jnp.zeros(plane, jnp.float32)
            for at, comp in enumerate((0, 2)):
                for z in levels:
                    column = ref[base + comp, z, :, edge_y : edge_y + 1]
                    packed = jnp.where(
                        lane == at * depth + z, jnp.broadcast_to(column, plane), packed
                    )
            send_y[stage, side] = packed

    def exchange(source, stage):
        low, high = pl.ds(0, 8), pl.ds(width - 8, 8)
        plan = (
            (source.at[pl.ds(0, 2), 0], halo_z.at[stage, 0], {"gz": -1}),
            (state_ref.at[pl.ds(3, 2), depth - 1], halo_z.at[stage, 1], {"gz": 1}),
            (source.at[2, depth - 1], edge_zy.at[stage], {"gz": 1, "gy": -1}),
            (source.at[2, depth - 1, low], edge_zx.at[stage], {"gz": 1, "gx": -1}),
            (source.at[0, 0, high], edge_xz.at[stage], {"gx": 1, "gz": -1}),
            (source.at[1, 0], edge_yz.at[stage], {"gy": 1, "gz": -1}),
            (send_x.at[stage, 0], halo_x.at[stage, 0], {"gx": -1}),
            (send_x.at[stage, 1], halo_x.at[stage, 1], {"gx": 1}),
            (send_y.at[stage, 0], halo_y.at[stage, 0], {"gy": -1}),
            (send_y.at[stage, 1], halo_y.at[stage, 1], {"gy": 1}),
            (source.at[0, :, high], edge_xy.at[stage], {"gx": 1, "gy": -1}),
            (source.at[1, :, low], edge_yx.at[stage], {"gy": 1, "gx": -1}),
        )
        out = []
        for number, (src, dst, move) in enumerate(plan):
            sends = takes = None
            for axis, by in move.items():
                last = counts[AXES.index(axis)] - 1
                up, down = place[axis] < last, place[axis] > 0
                send, take = (up, down) if by > 0 else (down, up)
                sends = send if sends is None else jnp.logical_and(sends, send)
                takes = take if takes is None else jnp.logical_and(takes, take)
            copy = pltpu.make_async_remote_copy(
                src_ref=src,
                dst_ref=dst,
                send_sem=send_sem.at[stage, number],
                recv_sem=recv_sem.at[stage, number],
                device_id={axis: place[axis] + by for axis, by in move.items()},
                device_id_type=MESH,
            )
            pl.when(sends)(copy.start)
            out.append((copy, dst, sends, takes))
        return out

    def land(copies):
        for copy, dst, sends, takes in copies:
            pl.when(takes)(copy.wait_recv)

            @pl.when(jnp.logical_not(takes))
            def _():
                dst[...] = jnp.zeros(dst.shape, jnp.float32)

        for copy, dst, sends, takes in copies:
            pl.when(sends)(copy.wait_send)

    def spread_row(line):
        return jnp.broadcast_to(line, plane)

    def complete(source, stage):
        half = COURANT
        last_row, last_lane = row == width - 1, lane == height - 1
        column = [[None] * depth for _ in range(4)]
        line = [[None] * depth for _ in range(4)]
        for k in range(2):
            for z in levels:
                n = k * depth + z
                for side in range(2):
                    column[2 * side + k][z] = jnp.broadcast_to(
                        halo_y[stage, side, :, n : n + 1], plane
                    )
                    line[2 * side + k][z] = halo_x[stage, side, n : n + 1, :]
        hx, hy, hz = ([state_ref[3 + c, z] for z in levels] for c in range(3))
        top = depth - 1
        for z in levels:
            ey_x, ez_x = spread_row(line[0][z]), spread_row(line[1][z])
            ex_y, ez_y = column[0][z], column[1][z]
            hx[z] = hx[z] - jnp.where(last_lane, half * ez_y, 0.0)
            hy[z] = hy[z] + jnp.where(last_row, half * ez_x, 0.0)
            hz[z] = hz[z] + (
                jnp.where(last_lane, half * ex_y, 0.0) - jnp.where(last_row, half * ey_x, 0.0)
            )
        hx[top] = hx[top] + half * halo_z[stage, 0, 1]
        hy[top] = hy[top] - half * halo_z[stage, 0, 0]
        for z in levels:
            state_ref[3, z] = hx[z]
            state_ref[4, z] = hy[z]
            state_ref[5, z] = hz[z]
        in_z = jnp.where(at_z > 0, half, 0.0)
        in_x = jnp.where(at_x > 0, half, 0.0)
        in_y = jnp.where(at_y > 0, half, 0.0)
        first = edge_zy[stage, :, 0:1]
        hx_z = (
            halo_z[stage, 1, 0]
            + in_z * source[1, 0]
            - jnp.where(last_lane, half * jnp.broadcast_to(first, plane), 0.0)
        )
        hy_z = (
            halo_z[stage, 1, 1]
            - in_z * source[0, 0]
            + jnp.where(last_row, half * spread_row(edge_zx[stage, 0:1, :]), 0.0)
        )
        lane_row = iota((1, height), 1)
        hy_x, hz_x = [], []
        for z in levels:
            low_y = line[2][z] + in_x * source[2, z, 0:1, :]
            if z == top:
                low_y = low_y - half * edge_xz[stage, 7:8, :]
            corner = jnp.broadcast_to(edge_xy[stage, z, 7:8, 0:1], (1, height))
            low_z = (
                line[3][z]
                - in_x * source[1, z, 0:1, :]
                + jnp.where(lane_row == height - 1, half * corner, 0.0)
            )
            hy_x.append(spread_row(low_y))
            hz_x.append(spread_row(low_z))
        hx_y, hz_y = [], []
        for z in levels:
            low_x = column[2][z] - in_y * jnp.broadcast_to(source[2, z, :, 0:1], plane)
            if z == top:
                final = edge_yz[stage, :, height - 1 : height]
                low_x = low_x + half * jnp.broadcast_to(final, plane)
            corner = jnp.broadcast_to(edge_yx[stage, z, 0:1, height - 1 : height], plane)
            low_z = (
                column[3][z]
                + in_y * jnp.broadcast_to(source[0, z, :, 0:1], plane)
                - jnp.where(last_row, half * corner, 0.0)
            )
            hx_y.append(low_x)
            hz_y.append(low_z)

        def before_x(field, edge):
            return [jnp.where(row == 0, e, pltpu.roll(f, 1, 0)) for f, e in zip(field, edge)]

        def before_y(field, edge):
            return [jnp.where(lane == 0, e, pltpu.roll(f, 1, 1)) for f, e in zip(field, edge)]

        hx_z, hy_z = [hx_z] + hx[:-1], [hy_z] + hy[:-1]
        hy_x, hz_x = before_x(hy, hy_x), before_x(hz, hz_x)
        hx_y, hz_y = before_y(hx, hx_y), before_y(hz, hz_y)
        for z in levels:
            curl = (
                (hz[z] - hz_y[z]) - (hy[z] - hy_z[z]),
                (hx[z] - hx_z[z]) - (hz[z] - hz_x[z]),
                (hy[z] - hy_x[z]) - (hx[z] - hx_y[z]),
            )
            for c in range(3):
                state_ref[c, z] = keep[z] * source[c, z] + gain[z] * curl[c]

    tile_x, tile_y = width // BLOCK, height // BLOCK
    spots = tile_x * tile_y
    freqs = wave_ref.shape[0]
    columns = 2 * freqs * dirs

    def steering():
        spot = iota((1, columns), 1)
        spot_d = spot % dirs
        spot_f = (spot // dirs) % freqs
        base = ((at_x * n_gy + at_y) * n_gz + at_z) * dirs
        polar = jnp.zeros((1, columns), jnp.float32)
        azimuth = jnp.zeros((1, columns), jnp.float32)
        wave = jnp.zeros((1, columns), jnp.float32)
        for d in range(dirs):
            polar = jnp.where(spot_d == d, angles_ref[0, base + d], polar)
            azimuth = jnp.where(spot_d == d, angles_ref[1, base + d], azimuth)
        for f in range(freqs):
            wave = jnp.where(spot_f == f, wave_ref[f], wave)
        unit_x = jnp.sin(polar) * jnp.cos(azimuth)
        unit_y = jnp.sin(polar) * jnp.sin(azimuth)
        unit_z = jnp.cos(polar)
        return wave, unit_x, unit_y, unit_z, spot

    def offset_table(steer):
        wave, unit_x, unit_y, unit_z, spot = steer
        cell = iota((spots, columns), 0)
        offset_x = (cell // tile_y).astype(jnp.float32)
        offset_y = (cell % tile_y).astype(jnp.float32)
        phase = wave * (unit_x * offset_x + unit_y * offset_y)
        quarter = jnp.where(spot >= columns // 2, math.pi / 2, 0.0)
        return jnp.cos(phase - quarter).astype(jnp.bfloat16)

    def tile_phases(steer):
        wave, unit_x, unit_y, unit_z, spot = steer
        tile = iota((total, columns), 0)
        start_z = (tile // (n_gx * n_gy)).astype(jnp.float32)
        start_x = ((tile // n_gy) % n_gx * tile_x).astype(jnp.float32)
        start_y = (tile % n_gy * tile_y).astype(jnp.float32)
        phase = wave * (unit_x * start_x + unit_y * start_y + unit_z * start_z)
        return jnp.cos(phase), jnp.sin(phase)

    loads[0].wait()
    magnetic_inside(fields_ref)
    pack_faces(fields_ref, 0)
    pl.semaphore_wait(barrier, total - 1)
    copies = exchange(fields_ref, 0)
    for load in loads[1:]:
        load.wait()
    material = material_ref[...]
    loss = jnp.zeros(material.shape, jnp.float32)
    eps = jnp.zeros(material.shape, jnp.float32)
    for label in range(eps_ref.shape[0]):
        chosen = material == label
        loss = jnp.where(chosen, loss_ref[label], loss)
        eps = jnp.where(chosen, eps_ref[label], eps)
    keep = (1.0 - loss) / (1.0 + loss)
    gain = COURANT / (eps * (1.0 + loss))
    steer = steering()
    turn_cos, turn_sin = tile_phases(steer)
    land(copies)
    complete(fields_ref, 0)
    old_ref = fields_ref
    for c in range(6):
        old_ref[c] = state_ref[c]
    magnetic_inside(old_ref)
    pack_faces(old_ref, 1)
    copies = exchange(old_ref, 1)
    masks = faces_ref[...].astype(jnp.float32)
    table = offset_table(steer)
    land(copies)
    complete(old_ref, 1)

    parts = (
        (5, 0, -1.0), (4, 0, 1.0), (2, 0, 1.0), (1, 0, -1.0),
        (5, 1, 1.0), (3, 1, -1.0), (2, 1, -1.0), (0, 1, 1.0),
        (4, 2, -1.0), (3, 2, 1.0), (1, 2, 1.0), (0, 2, -1.0),
    )
    sums = []
    for comp, normal, sign in parts:
        one = state_ref[comp, 0] * masks[normal, 0]
        for z in range(1, depth):
            one = one + state_ref[comp, z] * masks[normal, z]
        sums.append(one * (sign / BLOCK**3))
    stacked = jnp.concatenate(sums, axis=0)
    take = (iota((height, spots), 1) % tile_y == iota((height, spots), 0) // BLOCK)
    spread = split_dot(stacked, take.astype(jnp.float32).astype(jnp.bfloat16))
    own = iota((width, spots), 1) // tile_y == iota((width, spots), 0) // BLOCK
    own_rows = [
        jnp.sum(
            jnp.where(own, spread[c * width : (c + 1) * width], 0.0), axis=0, keepdims=True
        )
        for c in range(CHANNELS)
    ]
    own_rows.append(jnp.zeros((ROWS - CHANNELS, spots), jnp.float32))
    gathered[me] = jnp.concatenate(own_rows, axis=0).astype(jnp.bfloat16)

    def rows_copy(slot, other):
        return pltpu.make_async_remote_copy(
            src_ref=gathered.at[slot],
            dst_ref=gathered.at[slot],
            send_sem=rows_send_sem.at[other],
            recv_sem=rows_recv_sem.at[slot],
            device_id=coords(other),
            device_id_type=MESH,
        )

    def send_rows(step, carry):
        rows_copy(me, (me + step) % total).start()
        return carry

    def take_rows(step, carry):
        other = (me + step) % total
        rows_copy(other, other).wait_recv()
        rows_copy(me, other).wait_send()
        return carry

    lax.fori_loop(1, total, send_rows, 0)
    lax.fori_loop(1, total, take_rows, 0)

    grid = jnp.dot(
        gathered[...].reshape(total * ROWS, spots), table, preferred_element_type=jnp.float32
    ).reshape(total, ROWS, columns)
    by_cos = jnp.sum(grid * turn_cos[:, None, :], axis=0)
    by_sin = jnp.sum(grid * turn_sin[:, None, :], axis=0)
    half = columns // 2
    crossed = pltpu.roll(by_sin, half, 1)
    column = iota((ROWS, columns), 1)
    joined = jnp.where(column < half, by_cos - crossed, by_cos + crossed)
    scale = 8.0 / math.sqrt(total * spots)
    turned = jnp.transpose(joined * scale)
    for k in range(2 * freqs):
        far_ref[:, k * CHANNELS : (k + 1) * CHANNELS] = turned[k * dirs : (k + 1) * dirs, :CHANNELS]


def shards(counts, fields, material, faces, permittivity, losses, angles, wavenumbers):
    total = math.prod(counts)
    depth, width, height = fields.shape[1:]
    dirs = angles.shape[1] // total
    freqs = wavenumbers.shape[0]
    spots = (width // BLOCK) * (height // BLOCK)
    vmem = pl.BlockSpec(memory_space=pltpu.VMEM)
    return pl.pallas_call(
        functools.partial(kernel, counts, dirs),
        out_shape=(
            jax.ShapeDtypeStruct(fields.shape, jnp.float32),
            jax.ShapeDtypeStruct((dirs, 2 * freqs * CHANNELS), jnp.float32),
        ),
        in_specs=[pl.BlockSpec(memory_space=pl.ANY)] * 7,
        out_specs=(vmem, vmem),
        scratch_shapes=[
            pltpu.VMEM(fields.shape, jnp.float32),
            pltpu.VMEM(material.shape, jnp.int32),
            pltpu.VMEM(faces.shape, jnp.int32),
            pltpu.SMEM(permittivity.shape, jnp.float32),
            pltpu.SMEM(losses.shape, jnp.float32),
            pltpu.SMEM(angles.shape, jnp.float32),
            pltpu.SMEM(wavenumbers.shape, jnp.float32),
            pltpu.VMEM((2, 2, 2 * depth, height), jnp.float32),
            pltpu.VMEM((2, 2, width, height), jnp.float32),
            pltpu.VMEM((2, 2, 2, width, height), jnp.float32),
            pltpu.VMEM((2, 2, 2 * depth, height), jnp.float32),
            pltpu.VMEM((2, 2, width, height), jnp.float32),
            pltpu.VMEM((2, width, height), jnp.float32),
            pltpu.VMEM((2, 8, height), jnp.float32),
            pltpu.VMEM((2, 8, height), jnp.float32),
            pltpu.VMEM((2, depth, 8, height), jnp.float32),
            pltpu.VMEM((2, width, height), jnp.float32),
            pltpu.VMEM((2, depth, 8, height), jnp.float32),
            pltpu.VMEM((total, ROWS, spots), jnp.bfloat16),
            pltpu.SemaphoreType.DMA((7,)),
            pltpu.SemaphoreType.DMA((2, 12)),
            pltpu.SemaphoreType.DMA((2, 12)),
            pltpu.SemaphoreType.DMA((total,)),
            pltpu.SemaphoreType.DMA((total,)),
        ],
        compiler_params=pltpu.CompilerParams(
            collective_id=0, has_side_effects=True, vmem_limit_bytes=48 * 1024 * 1024
        ),
    )(fields, material, faces, permittivity, losses, angles, wavenumbers)


def solution(mesh):
    counts = tuple(mesh.shape[axis] for axis in AXES)
    return jax.shard_map(
        functools.partial(shards, counts),
        mesh=mesh,
        in_specs=(
            P(None, "gz", "gx", "gy"),
            P("gz", "gx", "gy"),
            P(None, "gz", "gx", "gy"),
            P(),
            P(),
            P(),
            P(),
        ),
        out_specs=(P(None, "gz", "gx", "gy"), P(("gx", "gy", "gz"), None)),
        check_vma=False,
    )
```

time: 32.1 us -> 27.7 us (0.86)
  Pallas kernels: 24.6 us -> 20.3 us
    pallas_call x1, Pallas kernels: 24.6 us -> 20.3 us  [shards(): pl.pallas_call(functools.partial(kernel, counts, dirs), out_shape=(jax.Sh...]
where the time goes in v2:
time: 27.7 us; the launch traced here: 27.4 us
  Pallas kernels  20.3 us (73%)
  local copies, waits for them, and re-layouts  6.5 us (23%)
  between operations  0.66 us (2%)
    pallas_call x1, Pallas kernels, shards(): pl.pallas_call(functools.partial(kernel, counts, dirs), out_shape=(jax.Sh...  20.3 us
    unnamed x16, local copies, waits for them, and re-layouts  6.5 us

profile of v2, /device:TPU:0, one launch (start us, length us, event | category | flops | bytes accessed | tf_op | source)
XLA Modules:
  0.0 27.4 jit_solution(13752140473139948536)
XLA Ops:
  0.6 0.0 copy-start
  0.6 0.9 %copy-done = f32[6,4,16,128]{3,2,1,0:T(8,128)S(1)} copy-done((f32[6,4,16,128]{3,2,1,0:T(8,128)S(1)}, f32[6,4,16,128]{3,2,1,0:T(8,128)}, u32[]{:S(2)}) %copy-start) | copy-done | bytes 196632
  1.6 0.0 copy-start.1
  1.6 0.9 %copy-done.1 = s32[3,4,16,128]{3,2,1,0:T(8,128)S(1)} copy-done((s32[3,4,16,128]{3,2,1,0:T(8,128)S(1)}, s32[3,4,16,128]{3,2,1,0:T(8,128)}, u32[]{:S(2)}) %copy-start.1) | copy-done | bytes 98328
  2.5 0.0 copy-start.2
  2.5 0.8 %copy-done.2 = s32[4,16,128]{2,1,0:T(8,128)S(1)} copy-done((s32[4,16,128]{2,1,0:T(8,128)S(1)}, s32[4,16,128]{2,1,0:T(8,128)}, u32[]{:S(2)}) %copy-start.2) | copy-done | bytes 32792
  3.2 0.0 copy-start.3
  3.2 0.7 %copy-done.3 = f32[2,512]{1,0:T(2,128)S(1)} copy-done((f32[2,512]{1,0:T(2,128)S(1)}, f32[2,512]{1,0:T(2,128)}, u32[]{:S(2)}) %copy-start.3) | copy-done | bytes 4120
  3.9 0.0 copy-start.4
  3.9 0.7 %copy-done.4 = f32[16]{0:T(128)S(1)} copy-done((f32[16]{0:T(128)S(1)}, f32[16]{0:T(128)}, u32[]{:S(2)}) %copy-start.4) | copy-done | bytes 88
  4.6 0.0 copy-start.5
  4.6 0.7 %copy-done.5 = f32[16]{0:T(128)S(1)} copy-done((f32[16]{0:T(128)S(1)}, f32[16]{0:T(128)}, u32[]{:S(2)}) %copy-start.5) | copy-done | bytes 88
  5.2 0.0 copy-start.6
  5.2 0.7 %copy-done.6 = f32[4]{0:T(128)S(1)} copy-done((f32[4]{0:T(128)S(1)}, f32[4]{0:T(128)}, u32[]{:S(2)}) %copy-start.6) | copy-done | bytes 40
  5.9 20.3 %shard_map.86 = (f32[6,4,16,128]{3,2,1,0:T(8,128)S(1)}, f32[16,96]{1,0:T(8,128)S(1)}) custom-call(f32[6,4,16,128]{3,2,1,0:T(8,128)S(1)} %copy-done, s32[4,16,128]{2,1,0:T(8,128)S(1)} %copy-done.2, s32[3,4,16,128]{3,2,1,0:T(8,128)S(1)} %copy-done.1, f32[16]{0:T(128)S(1)} %copy-done.4, f32[16]{0:T(128)S(1)} %copy-done.5, f32[2,512]{1,0:T(2,128)S(1)} %copy-done.3, ...), custom_call_target="tpu_custom_call" | custom-call | tf_op jit(solution)/shard_map/pallas_call | solution.py:431
  26.1 0.7 %copy.11 = f32[6,4,16,128]{3,2,1,0:T(8,128)} copy(f32[6,4,16,128]{3,2,1,0:T(8,128)S(1)} %get-tuple-element.4) | data formatting | bytes 393216
  26.8 0.6 %copy.12 = f32[16,96]{1,0:T(8,128)} copy(f32[16,96]{1,0:T(8,128)S(1)} %get-tuple-element.5) | data formatting | bytes 12288
Async XLA Ops:
  0.6 0.9 %copy-start = (f32[6,4,16,128]{3,2,1,0:T(8,128)S(1)}, f32[6,4,16,128]{3,2,1,0:T(8,128)}, u32[]{:S(2)}) copy-start(f32[6,4,16,128]{3,2,1,0:T(8,128)} %fields_hbm.1) | copy-start | bytes 589828
  1.6 0.9 %copy-start.1 = (s32[3,4,16,128]{3,2,1,0:T(8,128)S(1)}, s32[3,4,16,128]{3,2,1,0:T(8,128)}, u32[]{:S(2)}) copy-start(s32[3,4,16,128]{3,2,1,0:T(8,128)} %faces_hbm.1) | copy-start | bytes 294916
  2.5 0.8 %copy-start.2 = (s32[4,16,128]{2,1,0:T(8,128)S(1)}, s32[4,16,128]{2,1,0:T(8,128)}, u32[]{:S(2)}) copy-start(s32[4,16,128]{2,1,0:T(8,128)} %material_hbm.1) | copy-start | bytes 98308
  3.2 0.7 %copy-start.3 = (f32[2,512]{1,0:T(2,128)S(1)}, f32[2,512]{1,0:T(2,128)}, u32[]{:S(2)}) copy-start(f32[2,512]{1,0:T(2,128)} %angles_hbm.1) | copy-start | bytes 12292
  3.9 0.7 %copy-start.4 = (f32[16]{0:T(128)S(1)}, f32[16]{0:T(128)}, u32[]{:S(2)}) copy-start(f32[16]{0:T(128)} %eps_hbm.1) | copy-start | bytes 196
  4.6 0.7 %copy-start.5 = (f32[16]{0:T(128)S(1)}, f32[16]{0:T(128)}, u32[]{:S(2)}) copy-start(f32[16]{0:T(128)} %loss_hbm.1) | copy-start | bytes 196
  5.2 0.7 %copy-start.6 = (f32[4]{0:T(128)S(1)}, f32[4]{0:T(128)}, u32[]{:S(2)}) copy-start(f32[4]{0:T(128)} %wave_hbm.1) | copy-start | bytes 52

commit v3 on v2

--- a/solution.py
+++ b/solution.py
@@ -38,8 +38,9 @@
     loss_hbm,
     angles_hbm,
     wave_hbm,
+    state_hbm,
+    far_ref,
     state_ref,
-    far_ref,
     fields_ref,
     material_ref,
     faces_ref,
@@ -71,12 +72,31 @@
     at_z, at_x, at_y = (place[axis] for axis in AXES)
     me = (at_z * n_gx + at_x) * n_gy + at_y
 
-    def coords(number):
-        return {
-            "gz": number // (n_gx * n_gy),
-            "gx": (number // n_gy) % n_gx,
-            "gy": number % n_gy,
-        }
+    def wrapped(at, by, count):
+        moved = at + by
+        return jnp.where(moved >= count, moved - count, moved)
+
+    def each_partner(act):
+        near = [
+            (dx, wrapped(at_x, dx, n_gx), dy, wrapped(at_y, dy, n_gy))
+            for dx in range(n_gx)
+            for dy in range(n_gy)
+        ]
+
+        def level(dz):
+            other_z = wrapped(at_z, dz, n_gz)
+            for dx, other_x, dy, other_y in near:
+                if isinstance(dz, int) and dz == dx == dy == 0:
+                    continue
+                number = (other_z * n_gx + other_x) * n_gy + other_y
+                act({"gz": other_z, "gx": other_x, "gy": other_y}, number)
+
+        if n_gz <= 4:
+            for dz in sorted(range(1, n_gz), key=lambda dz: abs(2 * dz - n_gz)):
+                level(dz)
+        else:
+            pl.loop(1, n_gz)(level)
+        level(0)
 
     pairs = (
         (fields_hbm, fields_ref),
@@ -93,13 +113,10 @@
 
     barrier = pltpu.get_barrier_semaphore()
 
-    def greet(step, carry):
-        pl.semaphore_signal(
-            barrier, inc=1, device_id=coords((me + step) % total), device_id_type=MESH
-        )
-        return carry
-
-    lax.fori_loop(1, total, greet, 0)
+    def greet(other, number):
+        pl.semaphore_signal(barrier, inc=1, device_id=other, device_id_type=MESH)
+
+    each_partner(greet)
 
     depth, width, height = fields_ref.shape[1:]
     plane = (width, height)
@@ -359,6 +376,9 @@
     land(copies)
     complete(old_ref, 1)
 
+    save = pltpu.make_async_copy(state_ref, state_hbm, local_sem.at[len(pairs)])
+    save.start()
+
     parts = (
         (5, 0, -1.0), (4, 0, 1.0), (2, 0, 1.0), (1, 0, -1.0),
         (5, 1, 1.0), (3, 1, -1.0), (2, 1, -1.0), (0, 1, 1.0),
@@ -383,28 +403,24 @@
     own_rows.append(jnp.zeros((ROWS - CHANNELS, spots), jnp.float32))
     gathered[me] = jnp.concatenate(own_rows, axis=0).astype(jnp.bfloat16)
 
-    def rows_copy(slot, other):
+    def rows_copy(slot, other, number):
         return pltpu.make_async_remote_copy(
             src_ref=gathered.at[slot],
             dst_ref=gathered.at[slot],
-            send_sem=rows_send_sem.at[other],
+            send_sem=rows_send_sem.at[number],
             recv_sem=rows_recv_sem.at[slot],
-            device_id=coords(other),
+            device_id=other,
             device_id_type=MESH,
         )
 
-    def send_rows(step, carry):
-        rows_copy(me, (me + step) % total).start()
-        return carry
-
-    def take_rows(step, carry):
-        other = (me + step) % total
-        rows_copy(other, other).wait_recv()
-        rows_copy(me, other).wait_send()
-        return carry
-
-    lax.fori_loop(1, total, send_rows, 0)
-    lax.fori_loop(1, total, take_rows, 0)
+    def take_rows(other, number):
+        rows_copy(number, other, number).wait_recv()
+
+    def end_rows(other, number):
+        rows_copy(me, other, number).wait_send()
+
+    each_partner(lambda other, number: rows_copy(me, other, number).start())
+    each_partner(take_rows)
 
     grid = jnp.dot(
         gathered[...].reshape(total * ROWS, spots), table, preferred_element_type=jnp.float32
@@ -419,6 +435,31 @@
     turned = jnp.transpose(joined * scale)
     for k in range(2 * freqs):
         far_ref[:, k * CHANNELS : (k + 1) * CHANNELS] = turned[k * dirs : (k + 1) * dirs, :CHANNELS]
+    each_partner(end_rows)
+    save.wait()
+
+
+def hand_over(*results):
+    count = len(results)
+
+    def body(*refs):
+        sems = refs[2 * count]
+        copies = [
+            pltpu.make_async_copy(refs[k], refs[count + k], sems.at[k]) for k in range(count)
+        ]
+        for copy in copies:
+            copy.start()
+        for copy in copies:
+            copy.wait()
+
+    return pl.pallas_call(
+        body,
+        out_shape=tuple(jax.ShapeDtypeStruct(r.shape, r.dtype) for r in results),
+        in_specs=[pl.BlockSpec(memory_space=pltpu.HBM)] * count,
+        out_specs=(pl.BlockSpec(memory_space=pltpu.HBM),) * count,
+        scratch_shapes=[pltpu.SemaphoreType.DMA((count,))],
+        compiler_params=pltpu.CompilerParams(vmem_limit_bytes=60 * 1024 * 1024),
+    )(*results)
 
 
 def shards(counts, fields, material, faces, permittivity, losses, angles, wavenumbers):
@@ -428,15 +469,16 @@
     freqs = wavenumbers.shape[0]
     spots = (width // BLOCK) * (height // BLOCK)
     vmem = pl.BlockSpec(memory_space=pltpu.VMEM)
-    return pl.pallas_call(
+    results = pl.pallas_call(
         functools.partial(kernel, counts, dirs),
         out_shape=(
             jax.ShapeDtypeStruct(fields.shape, jnp.float32),
             jax.ShapeDtypeStruct((dirs, 2 * freqs * CHANNELS), jnp.float32),
         ),
-        in_specs=[pl.BlockSpec(memory_space=pl.ANY)] * 7,
-        out_specs=(vmem, vmem),
+        in_specs=[pl.BlockSpec(memory_space=pltpu.HBM)] * 7,
+        out_specs=(pl.BlockSpec(memory_space=pltpu.HBM), vmem),
         scratch_shapes=[
+            pltpu.VMEM(fields.shape, jnp.float32),
             pltpu.VMEM(fields.shape, jnp.float32),
             pltpu.VMEM(material.shape, jnp.int32),
             pltpu.VMEM(faces.shape, jnp.int32),
@@ -456,16 +498,17 @@
             pltpu.VMEM((2, width, height), jnp.float32),
             pltpu.VMEM((2, depth, 8, height), jnp.float32),
             pltpu.VMEM((total, ROWS, spots), jnp.bfloat16),
-            pltpu.SemaphoreType.DMA((7,)),
+            pltpu.SemaphoreType.DMA((8,)),
             pltpu.SemaphoreType.DMA((2, 12)),
             pltpu.SemaphoreType.DMA((2, 12)),
             pltpu.SemaphoreType.DMA((total,)),
             pltpu.SemaphoreType.DMA((total,)),
         ],
         compiler_params=pltpu.CompilerParams(
-            collective_id=0, has_side_effects=True, vmem_limit_bytes=48 * 1024 * 1024
+            collective_id=0, has_side_effects=True, vmem_limit_bytes=60 * 1024 * 1024
         ),
     )(fields, material, faces, permittivity, losses, angles, wavenumbers)
+    return hand_over(*results)
 
 
 def solution(mesh):

time: 27.7 us -> 28.1 us (1.014)
  Pallas kernels: 20.3 us -> 27.4 us
  local copies, waits for them, and re-layouts: 6.5 us -> 0 us
    pallas_call x0 -> x1, Pallas kernels: none -> 7.32 us  [hand_over(): pl.pallas_call(body, out_shape=tuple((jax.ShapeDtypeStruct(r.shape, r.dty...]
    unnamed x16 -> x0, local copies, waits for them, and re-layouts: 6.5 us -> none
where the time goes in v3:
time: 28.1 us; the launch traced here: 28 us
  Pallas kernels  27.4 us (98%)
  between operations  0.64 us (2%)
    pallas_call x1, Pallas kernels, shards(): pl.pallas_call(functools.partial(kernel, counts, dirs), out_shape=(jax.Sh...  20 us
    pallas_call x1, Pallas kernels, hand_over(): pl.pallas_call(body, out_shape=tuple((jax.ShapeDtypeStruct(r.shape, r.dty...  7.32 us

profile of v3, /device:TPU:0, one launch (start us, length us, event | category | flops | bytes accessed | tf_op | source)
XLA Modules:
  0.0 28.0 jit_solution(16965491957050141217)
XLA Ops:
  0.6 20.0 %shard_map.86 = (f32[6,4,16,128]{3,2,1,0:T(8,128)}, f32[16,96]{1,0:T(8,128)}) custom-call(f32[6,4,16,128]{3,2,1,0:T(8,128)} %fields_hbm.1, s32[4,16,128]{2,1,0:T(8,128)} %material_hbm.1, s32[3,4,16,128]{3,2,1,0:T(8,128)} %faces_hbm.1, f32[16]{0:T(128)} %eps_hbm.1, f32[16]{0:T(128)} %loss_hbm.1, f32[2,512]{1,0:T(2,128)} %angles_hbm.1, f32[4]{0:T(128)} %wave_hbm.1), custom_call_target="tpu_custom_call" | custom-call | tf_op jit(solution)/shard_map/pallas_call | solution.py:472
  20.7 7.3 %shard_map.87 = (f32[6,4,16,128]{3,2,1,0:T(8,128)}, f32[16,96]{1,0:T(8,128)}) custom-call(f32[6,4,16,128]{3,2,1,0:T(8,128)} %get-tuple-element.4.refs_0_, f32[16,96]{1,0:T(8,128)} %get-tuple-element.5.refs_1_), custom_call_target="tpu_custom_call" | custom-call | tf_op jit(solution)/shard_map/pallas_call | solution.py:455

commit v4 on v3

--- a/solution.py
+++ b/solution.py
@@ -26,6 +26,25 @@
     return jnp.dot(high, right, preferred_element_type=jnp.float32) + jnp.dot(
         low, right, preferred_element_type=jnp.float32
     )
+
+
+def sin_cos(angle):
+    turns = jnp.floor(angle * (2 / math.pi) + 0.5)
+    rest = angle - turns * 1.5703125
+    rest = rest - turns * 4.837512969970703125e-4
+    rest = rest - turns * 7.54978995489188216e-8
+    square = rest * rest
+    sine = -1.9515295891e-4 * square + 8.3321608736e-3
+    sine = (sine * square - 1.6666654611e-1) * square * rest + rest
+    cosine = 2.443315711809948e-5 * square - 1.388731625493765e-3
+    cosine = (cosine * square + 4.166664568298827e-2) * square * square - 0.5 * square + 1.0
+    quarter = turns.astype(jnp.int32)
+    odd = (quarter & 1) == 1
+    sin_out = jnp.where(odd, cosine, sine)
+    cos_out = jnp.where(odd, sine, cosine)
+    sin_out = jnp.where((quarter & 2) == 2, -sin_out, sin_out)
+    cos_out = jnp.where(((quarter + 1) & 2) == 2, -cos_out, cos_out)
+    return sin_out, cos_out
 
 
 def kernel(
@@ -60,43 +79,36 @@
     edge_yz,
     edge_yx,
     gathered,
+    table_ref,
+    part_out,
+    part_in,
     local_sem,
     send_sem,
     recv_sem,
     rows_send_sem,
     rows_recv_sem,
+    part_send_sem,
+    part_recv_sem,
 ):
     n_gz, n_gx, n_gy = counts
     total = n_gz * n_gx * n_gy
     place = {axis: lax.axis_index(axis) for axis in AXES}
     at_z, at_x, at_y = (place[axis] for axis in AXES)
-    me = (at_z * n_gx + at_x) * n_gy + at_y
+    me = at_x * n_gy + at_y
+    in_plane = n_gx * n_gy
 
     def wrapped(at, by, count):
         moved = at + by
         return jnp.where(moved >= count, moved - count, moved)
 
-    def each_partner(act):
-        near = [
-            (dx, wrapped(at_x, dx, n_gx), dy, wrapped(at_y, dy, n_gy))
-            for dx in range(n_gx)
-            for dy in range(n_gy)
-        ]
-
-        def level(dz):
-            other_z = wrapped(at_z, dz, n_gz)
-            for dx, other_x, dy, other_y in near:
-                if isinstance(dz, int) and dz == dx == dy == 0:
-                    continue
-                number = (other_z * n_gx + other_x) * n_gy + other_y
-                act({"gz": other_z, "gx": other_x, "gy": other_y}, number)
-
-        if n_gz <= 4:
-            for dz in sorted(range(1, n_gz), key=lambda dz: abs(2 * dz - n_gz)):
-                level(dz)
-        else:
-            pl.loop(1, n_gz)(level)
-        level(0)
+    def each_in_plane(act):
+        for dx in range(n_gx):
+            for dy in range(n_gy):
+                if dx or dy:
+                    other_x, other_y = wrapped(at_x, dx, n_gx), wrapped(at_y, dy, n_gy)
+                    act({"gx": other_x, "gy": other_y}, other_x * n_gy + other_y)
+
+    levels_away = sorted(range(1, n_gz), key=lambda dz: abs(2 * dz - n_gz))
 
     pairs = (
         (fields_hbm, fields_ref),
@@ -112,11 +124,29 @@
         load.start()
 
     barrier = pltpu.get_barrier_semaphore()
-
-    def greet(other, number):
-        pl.semaphore_signal(barrier, inc=1, device_id=other, device_id_type=MESH)
-
-    each_partner(greet)
+    each_in_plane(
+        lambda other, number: pl.semaphore_signal(
+            barrier, inc=1, device_id=other, device_id_type=MESH
+        )
+    )
+    for dz in levels_away:
+        pl.semaphore_signal(
+            barrier, inc=1, device_id={"gz": wrapped(at_z, dz, n_gz)}, device_id_type=MESH
+        )
+    greeted = n_gx * n_gy + n_gz - 2
+    for axis, last in (("gx", n_gx - 1), ("gy", n_gy - 1)):
+        for by in (-1, 1):
+            there = jnp.logical_and(
+                place["gz"] < n_gz - 1 if by > 0 else place["gz"] > 0,
+                place[axis] > 0 if by > 0 else place[axis] < last,
+            )
+            other = {"gz": place["gz"] + by, axis: place[axis] - by}
+
+            @pl.when(there)
+            def _():
+                pl.semaphore_signal(barrier, inc=1, device_id=other, device_id_type=MESH)
+
+            greeted = greeted + jnp.where(there, 1, 0)
 
     depth, width, height = fields_ref.shape[1:]
     plane = (width, height)
@@ -309,11 +339,11 @@
     freqs = wave_ref.shape[0]
     columns = 2 * freqs * dirs
 
-    def steering():
+    def steering(dz):
         spot = iota((1, columns), 1)
         spot_d = spot % dirs
         spot_f = (spot // dirs) % freqs
-        base = ((at_x * n_gy + at_y) * n_gz + at_z) * dirs
+        base = (me * n_gz + wrapped(at_z, dz, n_gz)) * dirs
         polar = jnp.zeros((1, columns), jnp.float32)
         azimuth = jnp.zeros((1, columns), jnp.float32)
         wave = jnp.zeros((1, columns), jnp.float32)
@@ -322,33 +352,39 @@
             azimuth = jnp.where(spot_d == d, angles_ref[1, base + d], azimuth)
         for f in range(freqs):
             wave = jnp.where(spot_f == f, wave_ref[f], wave)
-        unit_x = jnp.sin(polar) * jnp.cos(azimuth)
-        unit_y = jnp.sin(polar) * jnp.sin(azimuth)
-        unit_z = jnp.cos(polar)
-        return wave, unit_x, unit_y, unit_z, spot
-
-    def offset_table(steer):
-        wave, unit_x, unit_y, unit_z, spot = steer
-        cell = iota((spots, columns), 0)
-        offset_x = (cell // tile_y).astype(jnp.float32)
-        offset_y = (cell % tile_y).astype(jnp.float32)
-        phase = wave * (unit_x * offset_x + unit_y * offset_y)
+        sin_p, cos_p = sin_cos(polar)
+        sin_a, cos_a = sin_cos(azimuth)
+        unit_x, unit_y, unit_z = sin_p * cos_a, sin_p * sin_a, cos_p
+
+        highs = tile_y // 8
+        coarse = iota((tile_x * highs, columns), 0)
+        low = iota((8, columns), 0).astype(jnp.float32)
         quarter = jnp.where(spot >= columns // 2, math.pi / 2, 0.0)
-        return jnp.cos(phase - quarter).astype(jnp.bfloat16)
-
-    def tile_phases(steer):
-        wave, unit_x, unit_y, unit_z, spot = steer
-        tile = iota((total, columns), 0)
-        start_z = (tile // (n_gx * n_gy)).astype(jnp.float32)
-        start_x = ((tile // n_gy) % n_gx * tile_x).astype(jnp.float32)
+        sin_c, cos_c = sin_cos(
+            wave
+            * (
+                unit_x * (coarse // highs).astype(jnp.float32)
+                + unit_y * (coarse % highs * 8).astype(jnp.float32)
+            )
+            - quarter
+        )
+        sin_l, cos_l = sin_cos(wave * (unit_y * low))
+        table = [
+            cos_c[k : k + 1] * cos_l - sin_c[k : k + 1] * sin_l for k in range(tile_x * highs)
+        ]
+        table_ref[:, dz * columns : (dz + 1) * columns] = jnp.concatenate(table, axis=0).astype(
+            jnp.bfloat16
+        )
+        tile = iota((in_plane, columns), 0)
+        start_x = (tile // n_gy * tile_x).astype(jnp.float32)
         start_y = (tile % n_gy * tile_y).astype(jnp.float32)
-        phase = wave * (unit_x * start_x + unit_y * start_y + unit_z * start_z)
-        return jnp.cos(phase), jnp.sin(phase)
+        start_z = at_z.astype(jnp.float32)
+        return sin_cos(wave * (unit_x * start_x + unit_y * start_y + unit_z * start_z))
 
     loads[0].wait()
     magnetic_inside(fields_ref)
     pack_faces(fields_ref, 0)
-    pl.semaphore_wait(barrier, total - 1)
+    pl.semaphore_wait(barrier, greeted)
     copies = exchange(fields_ref, 0)
     for load in loads[1:]:
         load.wait()
@@ -361,8 +397,7 @@
         eps = jnp.where(chosen, eps_ref[label], eps)
     keep = (1.0 - loss) / (1.0 + loss)
     gain = COURANT / (eps * (1.0 + loss))
-    steer = steering()
-    turn_cos, turn_sin = tile_phases(steer)
+    turns = {dz: steering(dz) for dz in levels_away[: len(levels_away) // 2 + 1]}
     land(copies)
     complete(fields_ref, 0)
     old_ref = fields_ref
@@ -372,7 +407,9 @@
     pack_faces(old_ref, 1)
     copies = exchange(old_ref, 1)
     masks = faces_ref[...].astype(jnp.float32)
-    table = offset_table(steer)
+    for dz in range(n_gz):
+        if dz not in turns:
+            turns[dz] = steering(dz)
     land(copies)
     complete(old_ref, 1)
 
@@ -413,29 +450,53 @@
             device_id_type=MESH,
         )
 
-    def take_rows(other, number):
-        rows_copy(number, other, number).wait_recv()
-
-    def end_rows(other, number):
-        rows_copy(me, other, number).wait_send()
-
-    each_partner(lambda other, number: rows_copy(me, other, number).start())
-    each_partner(take_rows)
+    each_in_plane(lambda other, number: rows_copy(me, other, number).start())
+    each_in_plane(lambda other, number: rows_copy(number, other, number).wait_recv())
 
     grid = jnp.dot(
-        gathered[...].reshape(total * ROWS, spots), table, preferred_element_type=jnp.float32
-    ).reshape(total, ROWS, columns)
-    by_cos = jnp.sum(grid * turn_cos[:, None, :], axis=0)
-    by_sin = jnp.sum(grid * turn_sin[:, None, :], axis=0)
+        gathered[...].reshape(in_plane * ROWS, spots),
+        table_ref[...],
+        preferred_element_type=jnp.float32,
+    )
     half = columns // 2
-    crossed = pltpu.roll(by_sin, half, 1)
     column = iota((ROWS, columns), 1)
-    joined = jnp.where(column < half, by_cos - crossed, by_cos + crossed)
     scale = 8.0 / math.sqrt(total * spots)
-    turned = jnp.transpose(joined * scale)
+
+    def part(dz):
+        turn_sin, turn_cos = turns[dz]
+        own = grid[:, dz * columns : (dz + 1) * columns]
+        by_cos = by_sin = None
+        for tile in range(in_plane):
+            block = own[tile * ROWS : (tile + 1) * ROWS]
+            one, two = block * turn_cos[tile : tile + 1], block * turn_sin[tile : tile + 1]
+            by_cos = one if by_cos is None else by_cos + one
+            by_sin = two if by_sin is None else by_sin + two
+        crossed = pltpu.roll(by_sin, half, 1)
+        return jnp.where(column < half, by_cos - crossed, by_cos + crossed) * scale
+
+    def part_copy(dz):
+        return pltpu.make_async_remote_copy(
+            src_ref=part_out.at[dz - 1],
+            dst_ref=part_in.at[dz - 1],
+            send_sem=part_send_sem.at[dz - 1],
+            recv_sem=part_recv_sem.at[dz - 1],
+            device_id={"gz": wrapped(at_z, dz, n_gz)},
+            device_id_type=MESH,
+        )
+
+    for dz in levels_away:
+        part_out[dz - 1] = part(dz)
+        part_copy(dz).start()
+    far = part(0)
+    for dz in levels_away:
+        part_copy(dz).wait_recv()
+        far = far + part_in[dz - 1]
+    turned = jnp.transpose(far)
     for k in range(2 * freqs):
         far_ref[:, k * CHANNELS : (k + 1) * CHANNELS] = turned[k * dirs : (k + 1) * dirs, :CHANNELS]
-    each_partner(end_rows)
+    for dz in levels_away:
+        part_copy(dz).wait_send()
+    each_in_plane(lambda other, number: rows_copy(me, other, number).wait_send())
     save.wait()
 
 
@@ -443,21 +504,15 @@
     count = len(results)
 
     def body(*refs):
-        sems = refs[2 * count]
-        copies = [
-            pltpu.make_async_copy(refs[k], refs[count + k], sems.at[k]) for k in range(count)
-        ]
-        for copy in copies:
-            copy.start()
-        for copy in copies:
-            copy.wait()
-
+        for k in range(count):
+            refs[count + k][...] = refs[k][...]
+
+    vmem = pl.BlockSpec(memory_space=pltpu.VMEM)
     return pl.pallas_call(
         body,
         out_shape=tuple(jax.ShapeDtypeStruct(r.shape, r.dtype) for r in results),
-        in_specs=[pl.BlockSpec(memory_space=pltpu.HBM)] * count,
-        out_specs=(pl.BlockSpec(memory_space=pltpu.HBM),) * count,
-        scratch_shapes=[pltpu.SemaphoreType.DMA((count,))],
+        in_specs=[vmem] * count,
+        out_specs=(vmem,) * count,
         compiler_params=pltpu.CompilerParams(vmem_limit_bytes=60 * 1024 * 1024),
     )(*results)
 
@@ -467,6 +522,8 @@
     depth, width, height = fields.shape[1:]
     dirs = angles.shape[1] // total
     freqs = wavenumbers.shape[0]
+    n_gz, n_gx, n_gy = counts
+    columns = 2 * freqs * dirs
     spots = (width // BLOCK) * (height // BLOCK)
     vmem = pl.BlockSpec(memory_space=pltpu.VMEM)
     results = pl.pallas_call(
@@ -497,12 +554,17 @@
             pltpu.VMEM((2, depth, 8, height), jnp.float32),
             pltpu.VMEM((2, width, height), jnp.float32),
             pltpu.VMEM((2, depth, 8, height), jnp.float32),
-            pltpu.VMEM((total, ROWS, spots), jnp.bfloat16),
+            pltpu.VMEM((n_gx * n_gy, ROWS, spots), jnp.bfloat16),
+            pltpu.VMEM((spots, n_gz * columns), jnp.bfloat16),
+            pltpu.VMEM((max(n_gz - 1, 1), ROWS, columns), jnp.float32),
+            pltpu.VMEM((max(n_gz - 1, 1), ROWS, columns), jnp.float32),
             pltpu.SemaphoreType.DMA((8,)),
             pltpu.SemaphoreType.DMA((2, 12)),
             pltpu.SemaphoreType.DMA((2, 12)),
-            pltpu.SemaphoreType.DMA((total,)),
-            pltpu.SemaphoreType.DMA((total,)),
+            pltpu.SemaphoreType.DMA((n_gx * n_gy,)),
+            pltpu.SemaphoreType.DMA((n_gx * n_gy,)),
+            pltpu.SemaphoreType.DMA((max(n_gz - 1, 1),)),
+            pltpu.SemaphoreType.DMA((max(n_gz - 1, 1),)),
         ],
         compiler_params=pltpu.CompilerParams(
             collective_id=0, has_side_effects=True, vmem_limit_bytes=60 * 1024 * 1024

time: 28.1 us -> 23.2 us (0.83)
  Pallas kernels: 27.4 us -> 22.4 us
    pallas_call x1, Pallas kernels: 7.32 us -> 1.62 us  [hand_over(): pl.pallas_call(body, out_shape=tuple((jax.ShapeDtypeStruct(r.shape, r.dty...]
    pallas_call x1, Pallas kernels: 20 us -> 20.8 us  [shards(): pl.pallas_call(functools.partial(kernel, counts, dirs), out_shape=(jax.Sh...]
where the time goes in v4:
time: 23.2 us; the launch traced here: 23 us
  Pallas kernels  22.4 us (97%)
  between operations  0.64 us (3%)
    pallas_call x1, Pallas kernels, shards(): pl.pallas_call(functools.partial(kernel, counts, dirs), out_shape=(jax.Sh...  20.8 us
    pallas_call x1, Pallas kernels, hand_over(): pl.pallas_call(body, out_shape=tuple((jax.ShapeDtypeStruct(r.shape, r.dty...  1.62 us

profile of v4, /device:TPU:0, one launch (start us, length us, event | category | flops | bytes accessed | tf_op | source)
XLA Modules:
  0.0 23.0 jit_solution(11909881215701271115)
XLA Ops:
  0.6 20.8 %shard_map.86 = (f32[6,4,16,128]{3,2,1,0:T(8,128)}, f32[16,96]{1,0:T(8,128)}) custom-call(f32[6,4,16,128]{3,2,1,0:T(8,128)} %fields_hbm.1, s32[4,16,128]{2,1,0:T(8,128)} %material_hbm.1, s32[3,4,16,128]{3,2,1,0:T(8,128)} %faces_hbm.1, f32[16]{0:T(128)} %eps_hbm.1, f32[16]{0:T(128)} %loss_hbm.1, f32[2,512]{1,0:T(2,128)} %angles_hbm.1, f32[4]{0:T(128)} %wave_hbm.1), custom_call_target="tpu_custom_call" | custom-call | tf_op jit(solution)/shard_map/pallas_call | solution.py:529
  21.4 1.6 %shard_map.87 = (f32[6,4,16,128]{3,2,1,0:T(8,128)}, f32[16,96]{1,0:T(8,128)}) custom-call(f32[6,4,16,128]{3,2,1,0:T(8,128)} %get-tuple-element.4.refs_0_, f32[16,96]{1,0:T(8,128)} %get-tuple-element.5.refs_1_), custom_call_target="tpu_custom_call" | custom-call | tf_op jit(solution)/shard_map/pallas_call | solution.py:511

commit v5 on v4

--- a/solution.py
+++ b/solution.py
@@ -57,9 +57,10 @@
     loss_hbm,
     angles_hbm,
     wave_hbm,
-    state_hbm,
+    state_ref,
     far_ref,
-    state_ref,
+    mid_ref,
+    inner_ref,
     fields_ref,
     material_ref,
     faces_ref,
@@ -123,6 +124,10 @@
     for load in loads:
         load.start()
 
+    halos = (halo_z, halo_x, halo_y, edge_zy, edge_zx, edge_xz, edge_xy, edge_yz, edge_yx)
+    for halo in halos:
+        halo[...] = jnp.zeros(halo.shape, jnp.float32)
+
     barrier = pltpu.get_barrier_semaphore()
     each_in_plane(
         lambda other, number: pl.semaphore_signal(
@@ -160,7 +165,7 @@
     def later_y(field):
         return [jnp.where(lane == height - 1, 0.0, pltpu.roll(f, height - 1, 1)) for f in field]
 
-    def magnetic_inside(source):
+    def magnetic_inside(source, stage):
         ex, ey, ez = ([source[c, z] for z in levels] for c in range(3))
         none = jnp.zeros(plane, jnp.float32)
         ey_z, ex_z = ey[1:] + [none], ex[1:] + [none]
@@ -173,21 +178,21 @@
                 (ey_x[z] - ey[z]) - (ex_y[z] - ex[z]),
             )
             for c in range(3):
-                state_ref[3 + c, z] = source[3 + c, z] - COURANT * curl[c]
+                inner_ref[stage, c, z] = source[3 + c, z] - COURANT * curl[c]
 
     def pack_faces(source, stage):
-        for side, ref, base, edge_x, edge_y in (
-            (0, source, 0, 0, 0),
-            (1, state_ref, 3, width - 1, height - 1),
+        for side, ref, edge_x, edge_y in (
+            (0, source, 0, 0),
+            (1, inner_ref.at[stage], width - 1, height - 1),
         ):
             for at, comp in enumerate((1, 2)):
                 for z in levels:
                     k = at * depth + z
-                    send_x[stage, side, k : k + 1, :] = ref[base + comp, z, edge_x : edge_x + 1, :]
+                    send_x[stage, side, k : k + 1, :] = ref[comp, z, edge_x : edge_x + 1, :]
             packed = jnp.zeros(plane, jnp.float32)
             for at, comp in enumerate((0, 2)):
                 for z in levels:
-                    column = ref[base + comp, z, :, edge_y : edge_y + 1]
+                    column = ref[comp, z, :, edge_y : edge_y + 1]
                     packed = jnp.where(
                         lane == at * depth + z, jnp.broadcast_to(column, plane), packed
                     )
@@ -197,7 +202,7 @@
         low, high = pl.ds(0, 8), pl.ds(width - 8, 8)
         plan = (
             (source.at[pl.ds(0, 2), 0], halo_z.at[stage, 0], {"gz": -1}),
-            (state_ref.at[pl.ds(3, 2), depth - 1], halo_z.at[stage, 1], {"gz": 1}),
+            (inner_ref.at[stage, pl.ds(0, 2), depth - 1], halo_z.at[stage, 1], {"gz": 1}),
             (source.at[2, depth - 1], edge_zy.at[stage], {"gz": 1, "gy": -1}),
             (source.at[2, depth - 1, low], edge_zx.at[stage], {"gz": 1, "gx": -1}),
             (source.at[0, 0, high], edge_xz.at[stage], {"gx": 1, "gz": -1}),
@@ -234,17 +239,10 @@
         for copy, dst, sends, takes in copies:
             pl.when(takes)(copy.wait_recv)
 
-            @pl.when(jnp.logical_not(takes))
-            def _():
-                dst[...] = jnp.zeros(dst.shape, jnp.float32)
-
-        for copy, dst, sends, takes in copies:
-            pl.when(sends)(copy.wait_send)
-
     def spread_row(line):
         return jnp.broadcast_to(line, plane)
 
-    def complete(source, stage):
+    def complete(source, target, stage):
         half = COURANT
         last_row, last_lane = row == width - 1, lane == height - 1
         column = [[None] * depth for _ in range(4)]
@@ -257,7 +255,7 @@
                         halo_y[stage, side, :, n : n + 1], plane
                     )
                     line[2 * side + k][z] = halo_x[stage, side, n : n + 1, :]
-        hx, hy, hz = ([state_ref[3 + c, z] for z in levels] for c in range(3))
+        hx, hy, hz = ([inner_ref[stage, c, z] for z in levels] for c in range(3))
         top = depth - 1
         for z in levels:
             ey_x, ez_x = spread_row(line[0][z]), spread_row(line[1][z])
@@ -270,9 +268,9 @@
         hx[top] = hx[top] + half * halo_z[stage, 0, 1]
         hy[top] = hy[top] - half * halo_z[stage, 0, 0]
         for z in levels:
-            state_ref[3, z] = hx[z]
-            state_ref[4, z] = hy[z]
-            state_ref[5, z] = hz[z]
+            target[3, z] = hx[z]
+            target[4, z] = hy[z]
+            target[5, z] = hz[z]
         in_z = jnp.where(at_z > 0, half, 0.0)
         in_x = jnp.where(at_x > 0, half, 0.0)
         in_y = jnp.where(at_y > 0, half, 0.0)
@@ -332,7 +330,7 @@
                 (hy[z] - hy_x[z]) - (hx[z] - hx_y[z]),
             )
             for c in range(3):
-                state_ref[c, z] = keep[z] * source[c, z] + gain[z] * curl[c]
+                target[c, z] = keep[z] * source[c, z] + gain[z] * curl[c]
 
     tile_x, tile_y = width // BLOCK, height // BLOCK
     spots = tile_x * tile_y
@@ -382,10 +380,10 @@
         return sin_cos(wave * (unit_x * start_x + unit_y * start_y + unit_z * start_z))
 
     loads[0].wait()
-    magnetic_inside(fields_ref)
+    magnetic_inside(fields_ref, 0)
     pack_faces(fields_ref, 0)
     pl.semaphore_wait(barrier, greeted)
-    copies = exchange(fields_ref, 0)
+    first = exchange(fields_ref, 0)
     for load in loads[1:]:
         load.wait()
     material = material_ref[...]
@@ -398,23 +396,17 @@
     keep = (1.0 - loss) / (1.0 + loss)
     gain = COURANT / (eps * (1.0 + loss))
     turns = {dz: steering(dz) for dz in levels_away[: len(levels_away) // 2 + 1]}
-    land(copies)
-    complete(fields_ref, 0)
-    old_ref = fields_ref
-    for c in range(6):
-        old_ref[c] = state_ref[c]
-    magnetic_inside(old_ref)
-    pack_faces(old_ref, 1)
-    copies = exchange(old_ref, 1)
+    land(first)
+    complete(fields_ref, mid_ref, 0)
+    magnetic_inside(mid_ref, 1)
+    pack_faces(mid_ref, 1)
+    second = exchange(mid_ref, 1)
     masks = faces_ref[...].astype(jnp.float32)
     for dz in range(n_gz):
         if dz not in turns:
             turns[dz] = steering(dz)
-    land(copies)
-    complete(old_ref, 1)
-
-    save = pltpu.make_async_copy(state_ref, state_hbm, local_sem.at[len(pairs)])
-    save.start()
+    land(second)
+    complete(mid_ref, state_ref, 1)
 
     parts = (
         (5, 0, -1.0), (4, 0, 1.0), (2, 0, 1.0), (1, 0, -1.0),
@@ -488,6 +480,9 @@
         part_out[dz - 1] = part(dz)
         part_copy(dz).start()
     far = part(0)
+    for copy, dst, sends, takes in first + second:
+        pl.when(sends)(copy.wait_send)
+    each_in_plane(lambda other, number: rows_copy(me, other, number).wait_send())
     for dz in levels_away:
         part_copy(dz).wait_recv()
         far = far + part_in[dz - 1]
@@ -496,24 +491,28 @@
         far_ref[:, k * CHANNELS : (k + 1) * CHANNELS] = turned[k * dirs : (k + 1) * dirs, :CHANNELS]
     for dz in levels_away:
         part_copy(dz).wait_send()
-    each_in_plane(lambda other, number: rows_copy(me, other, number).wait_send())
-    save.wait()
 
 
 def hand_over(*results):
     count = len(results)
 
     def body(*refs):
-        for k in range(count):
-            refs[count + k][...] = refs[k][...]
-
-    vmem = pl.BlockSpec(memory_space=pltpu.VMEM)
+        sems = refs[2 * count]
+        copies = [
+            pltpu.make_async_copy(refs[k], refs[count + k], sems.at[k]) for k in range(count)
+        ]
+        for copy in copies:
+            copy.start()
+        for copy in copies:
+            copy.wait()
+
     return pl.pallas_call(
         body,
         out_shape=tuple(jax.ShapeDtypeStruct(r.shape, r.dtype) for r in results),
-        in_specs=[vmem] * count,
-        out_specs=(vmem,) * count,
-        compiler_params=pltpu.CompilerParams(vmem_limit_bytes=60 * 1024 * 1024),
+        in_specs=[pl.BlockSpec(memory_space=pl.ANY)] * count,
+        out_specs=(pl.BlockSpec(memory_space=pltpu.HBM),) * count,
+        scratch_shapes=[pltpu.SemaphoreType.DMA((count,))],
+        compiler_params=pltpu.CompilerParams(vmem_limit_bytes=1024 * 1024),
     )(*results)
 
 
@@ -529,13 +528,14 @@
     results = pl.pallas_call(
         functools.partial(kernel, counts, dirs),
         out_shape=(
-            jax.ShapeDtypeStruct(fields.shape, jnp.float32),
-            jax.ShapeDtypeStruct((dirs, 2 * freqs * CHANNELS), jnp.float32),
+            pltpu.VMEM(fields.shape, jnp.float32),
+            pltpu.VMEM((dirs, 2 * freqs * CHANNELS), jnp.float32),
         ),
         in_specs=[pl.BlockSpec(memory_space=pltpu.HBM)] * 7,
-        out_specs=(pl.BlockSpec(memory_space=pltpu.HBM), vmem),
+        out_specs=(vmem, vmem),
         scratch_shapes=[
             pltpu.VMEM(fields.shape, jnp.float32),
+            pltpu.VMEM((2, 3) + fields.shape[1:], jnp.float32),
             pltpu.VMEM(fields.shape, jnp.float32),
             pltpu.VMEM(material.shape, jnp.int32),
             pltpu.VMEM(faces.shape, jnp.int32),
@@ -558,7 +558,7 @@
             pltpu.VMEM((spots, n_gz * columns), jnp.bfloat16),
             pltpu.VMEM((max(n_gz - 1, 1), ROWS, columns), jnp.float32),
             pltpu.VMEM((max(n_gz - 1, 1), ROWS, columns), jnp.float32),
-            pltpu.SemaphoreType.DMA((8,)),
+            pltpu.SemaphoreType.DMA((7,)),
             pltpu.SemaphoreType.DMA((2, 12)),
             pltpu.SemaphoreType.DMA((2, 12)),
             pltpu.SemaphoreType.DMA((n_gx * n_gy,)),

time: 23.2 us -> 21.6 us (0.931)
  Pallas kernels: 22.4 us -> 20.8 us
    pallas_call x1, Pallas kernels: 1.62 us -> 0.7 us  [hand_over(): pl.pallas_call(body, out_shape=tuple((jax.ShapeDtypeStruct(r.shape, r.dty...]
    pallas_call x1, Pallas kernels: 20.8 us -> 20.1 us  [shards(): pl.pallas_call(functools.partial(kernel, counts, dirs), out_shape=(pltpu....]
where the time goes in v5:
time: 21.6 us; the launch traced here: 21.4 us
  Pallas kernels  20.8 us (96%)
  between operations  0.64 us (3%)
    pallas_call x1, Pallas kernels, shards(): pl.pallas_call(functools.partial(kernel, counts, dirs), out_shape=(pltpu....  20.1 us
    pallas_call x1, Pallas kernels, hand_over(): pl.pallas_call(body, out_shape=tuple((jax.ShapeDtypeStruct(r.shape, r.dty...  0.7 us

profile of v5, /device:TPU:0, one launch (start us, length us, event | category | flops | bytes accessed | tf_op | source)
XLA Modules:
  0.0 21.4 jit_solution(10820614019843555655)
XLA Ops:
  0.6 20.1 %shard_map.86 = (f32[6,4,16,128]{3,2,1,0:T(8,128)S(1)}, f32[16,96]{1,0:T(8,128)S(1)}) custom-call(f32[6,4,16,128]{3,2,1,0:T(8,128)} %fields_hbm.1, s32[4,16,128]{2,1,0:T(8,128)} %material_hbm.1, s32[3,4,16,128]{3,2,1,0:T(8,128)} %faces_hbm.1, f32[16]{0:T(128)} %eps_hbm.1, f32[16]{0:T(128)} %loss_hbm.1, f32[2,512]{1,0:T(2,128)} %angles_hbm.1, f32[4]{0:T(128)} %wave_hbm.1), custom_call_target="tpu_custom_call" | custom-call | tf_op jit(solution)/shard_map/pallas_call | solution.py:528
  20.7 0.7 %shard_map.87 = (f32[6,4,16,128]{3,2,1,0:T(8,128)}, f32[16,96]{1,0:T(8,128)}) custom-call(f32[6,4,16,128]{3,2,1,0:T(8,128)S(1)} %get-tuple-element.4.refs_0_, f32[16,96]{1,0:T(8,128)S(1)} %get-tuple-element.5.refs_1_), custom_call_target="tpu_custom_call" | custom-call | tf_op jit(solution)/shard_map/pallas_call | solution.py:509

commit v6 on v5

--- a/solution.py
+++ b/solution.py
@@ -121,8 +121,7 @@
         (faces_hbm, faces_ref),
     )
     loads = [pltpu.make_async_copy(a, b, local_sem.at[k]) for k, (a, b) in enumerate(pairs)]
-    for load in loads:
-        load.start()
+    loads[0].start()
 
     halos = (halo_z, halo_x, halo_y, edge_zy, edge_zx, edge_xz, edge_xy, edge_yz, edge_yx)
     for halo in halos:
@@ -152,6 +151,9 @@
                 pl.semaphore_signal(barrier, inc=1, device_id=other, device_id_type=MESH)
 
             greeted = greeted + jnp.where(there, 1, 0)
+
+    for load in loads[1:]:
+        load.start()
 
     depth, width, height = fields_ref.shape[1:]
     plane = (width, height)
@@ -395,16 +397,16 @@
         eps = jnp.where(chosen, eps_ref[label], eps)
     keep = (1.0 - loss) / (1.0 + loss)
     gain = COURANT / (eps * (1.0 + loss))
-    turns = {dz: steering(dz) for dz in levels_away[: len(levels_away) // 2 + 1]}
+    order = levels_away + [0]
+    shares = [order[0::4], order[1::4] + order[2::4], order[3::4]]
+    turns = {dz: steering(dz) for dz in shares[0]}
     land(first)
     complete(fields_ref, mid_ref, 0)
     magnetic_inside(mid_ref, 1)
     pack_faces(mid_ref, 1)
     second = exchange(mid_ref, 1)
     masks = faces_ref[...].astype(jnp.float32)
-    for dz in range(n_gz):
-        if dz not in turns:
-            turns[dz] = steering(dz)
+    turns.update({dz: steering(dz) for dz in shares[1]})
     land(second)
     complete(mid_ref, state_ref, 1)
 
@@ -443,6 +445,7 @@
         )
 
     each_in_plane(lambda other, number: rows_copy(me, other, number).start())
+    turns.update({dz: steering(dz) for dz in shares[2]})
     each_in_plane(lambda other, number: rows_copy(number, other, number).wait_recv())
 
     grid = jnp.dot(

time: 21.6 us -> 21.6 us (level)
  no operation moved by 1% of the time
where the time goes in v6:
time: 21.6 us; the launch traced here: 21.4 us
  Pallas kernels  20.8 us (96%)
  between operations  0.64 us (3%)
    pallas_call x1, Pallas kernels, shards(): pl.pallas_call(functools.partial(kernel, counts, dirs), out_shape=(pltpu....  20.1 us
    pallas_call x1, Pallas kernels, hand_over(): pl.pallas_call(body, out_shape=tuple((jax.ShapeDtypeStruct(r.shape, r.dty...  0.7 us

profile of v6, /device:TPU:0, one launch (start us, length us, event | category | flops | bytes accessed | tf_op | source)
XLA Modules:
  0.0 21.4 jit_solution(7438528210127796779)
XLA Ops:
  0.6 20.1 %shard_map.86 = (f32[6,4,16,128]{3,2,1,0:T(8,128)S(1)}, f32[16,96]{1,0:T(8,128)S(1)}) custom-call(f32[6,4,16,128]{3,2,1,0:T(8,128)} %fields_hbm.1, s32[4,16,128]{2,1,0:T(8,128)} %material_hbm.1, s32[3,4,16,128]{3,2,1,0:T(8,128)} %faces_hbm.1, f32[16]{0:T(128)} %eps_hbm.1, f32[16]{0:T(128)} %loss_hbm.1, f32[2,512]{1,0:T(2,128)} %angles_hbm.1, f32[4]{0:T(128)} %wave_hbm.1), custom_call_target="tpu_custom_call" | custom-call | tf_op jit(solution)/shard_map/pallas_call | solution.py:531
  20.7 0.7 %shard_map.87 = (f32[6,4,16,128]{3,2,1,0:T(8,128)}, f32[16,96]{1,0:T(8,128)}) custom-call(f32[6,4,16,128]{3,2,1,0:T(8,128)S(1)} %get-tuple-element.4.refs_0_, f32[16,96]{1,0:T(8,128)S(1)} %get-tuple-element.5.refs_1_), custom_call_target="tpu_custom_call" | custom-call | tf_op jit(solution)/shard_map/pallas_call | solution.py:512

commit v7 on v6

--- a/solution.py
+++ b/solution.py
@@ -182,11 +182,13 @@
             for c in range(3):
                 inner_ref[stage, c, z] = source[3 + c, z] - COURANT * curl[c]
 
-    def pack_faces(source, stage):
+    def pack_faces(source, stage, sides):
         for side, ref, edge_x, edge_y in (
             (0, source, 0, 0),
             (1, inner_ref.at[stage], width - 1, height - 1),
         ):
+            if side not in sides:
+                continue
             for at, comp in enumerate((1, 2)):
                 for z in levels:
                     k = at * depth + z
@@ -200,7 +202,7 @@
                     )
             send_y[stage, side] = packed
 
-    def exchange(source, stage):
+    def exchange(source, stage, sides):
         low, high = pl.ds(0, 8), pl.ds(width - 8, 8)
         plan = (
             (source.at[pl.ds(0, 2), 0], halo_z.at[stage, 0], {"gz": -1}),
@@ -218,6 +220,8 @@
         )
         out = []
         for number, (src, dst, move) in enumerate(plan):
+            if (1 if number in (1, 7, 9) else 0) not in sides:
+                continue
             sends = takes = None
             for axis, by in move.items():
                 last = counts[AXES.index(axis)] - 1
@@ -383,9 +387,9 @@
 
     loads[0].wait()
     magnetic_inside(fields_ref, 0)
-    pack_faces(fields_ref, 0)
+    pack_faces(fields_ref, 0, (0, 1))
     pl.semaphore_wait(barrier, greeted)
-    first = exchange(fields_ref, 0)
+    first = exchange(fields_ref, 0, (0, 1))
     for load in loads[1:]:
         load.wait()
     material = material_ref[...]
@@ -402,9 +406,11 @@
     turns = {dz: steering(dz) for dz in shares[0]}
     land(first)
     complete(fields_ref, mid_ref, 0)
+    pack_faces(mid_ref, 1, (0,))
+    second = exchange(mid_ref, 1, (0,))
     magnetic_inside(mid_ref, 1)
-    pack_faces(mid_ref, 1)
-    second = exchange(mid_ref, 1)
+    pack_faces(mid_ref, 1, (1,))
+    second = second + exchange(mid_ref, 1, (1,))
     masks = faces_ref[...].astype(jnp.float32)
     turns.update({dz: steering(dz) for dz in shares[1]})
     land(second)

time: 21.6 us -> 21.6 us (level)
  no operation moved by 1% of the time
where the time goes in v7:
time: 21.6 us; the launch traced here: 21.4 us
  Pallas kernels  20.8 us (96%)
  between operations  0.64 us (3%)
    pallas_call x1, Pallas kernels, shards(): pl.pallas_call(functools.partial(kernel, counts, dirs), out_shape=(pltpu....  20.1 us
    pallas_call x1, Pallas kernels, hand_over(): pl.pallas_call(body, out_shape=tuple((jax.ShapeDtypeStruct(r.shape, r.dty...  0.7 us

profile of v7, /device:TPU:0, one launch (start us, length us, event | category | flops | bytes accessed | tf_op | source)
XLA Modules:
  0.0 21.4 jit_solution(11936755860422899233)
XLA Ops:
  0.6 20.1 %shard_map.86 = (f32[6,4,16,128]{3,2,1,0:T(8,128)S(1)}, f32[16,96]{1,0:T(8,128)S(1)}) custom-call(f32[6,4,16,128]{3,2,1,0:T(8,128)} %fields_hbm.1, s32[4,16,128]{2,1,0:T(8,128)} %material_hbm.1, s32[3,4,16,128]{3,2,1,0:T(8,128)} %faces_hbm.1, f32[16]{0:T(128)} %eps_hbm.1, f32[16]{0:T(128)} %loss_hbm.1, f32[2,512]{1,0:T(2,128)} %angles_hbm.1, f32[4]{0:T(128)} %wave_hbm.1), custom_call_target="tpu_custom_call" | custom-call | tf_op jit(solution)/shard_map/pallas_call | solution.py:537
  20.7 0.7 %shard_map.87 = (f32[6,4,16,128]{3,2,1,0:T(8,128)}, f32[16,96]{1,0:T(8,128)}) custom-call(f32[6,4,16,128]{3,2,1,0:T(8,128)S(1)} %get-tuple-element.4.refs_0_, f32[16,96]{1,0:T(8,128)S(1)} %get-tuple-element.5.refs_1_), custom_call_target="tpu_custom_call" | custom-call | tf_op jit(solution)/shard_map/pallas_call | solution.py:518
